TPU v7x, 1024 devices: a whole 8x8x8 slice. The times are simulated.
1024 devices in a mesh: node: 32 (over y_lo, z, core), local: 32 (over y_hi, x).
Axes of the slice: x: 8, y: 8 (y_hi: 4, y_lo: 2; y = y_hi * 2 + y_lo), z: 8, core: 2. Of those that a mesh axis runs over, the one named last changes fastest.
Arguments:
- tokens: bfloat16 [131072, 12288], P(('node', 'local')), may hold values from -6 to 6
- weight_q: bfloat16 [64, 12288], P('local'), may hold values from -127 to 127
- weight_scale: bfloat16 [64, 48], P('local'), may hold values from 6.2942505e-05 to 0.00025177002
- cotangent: bfloat16 [131072, 64], P(('node', 'local')), may hold values from -6 to 6
Outputs:
- activation: bfloat16 [131072, 64], P(('node', 'local'))
- gradient: float32 [3072, 256], P(('node', 'local'))
All inputs are finite; a program needn't handle non-finite values. Where the computation divides by a largest or mean magnitude, that divisor is 1e-20 or more.
Results may differ from a plain program's by a relative error of at most 0.015.
Values may be sent and summed in bfloat16 or wider, within the bound.
No kernel may reach another device: no remote copies, remote signals or barrier semaphores. Data moves between devices by JAX's collectives and lax.ppermute only.
A program may use at most 32 MiB of HBM per device.

v0:
```python
import jax
import jax.numpy as jnp
from jax import lax
from jax.sharding import PartitionSpec as P

BLOCK = 256


EPSILON = 1e-06
CLIP_LEVEL = 3.0
TANH_SCALE = 0.7978845608028654
CUBIC_TERM = 0.044715


def gelu_value(before):
    inner = TANH_SCALE * (before + CUBIC_TERM * before * before * before)
    return 0.5 * before * (1.0 + jnp.tanh(inner))


def gelu_slope(before):
    tanh_inner = jnp.tanh(TANH_SCALE * (before + CUBIC_TERM * before * before * before))
    return 0.5 * (1.0 + tanh_inner) + 0.5 * before * (
        1.0 - tanh_inner * tanh_inner
    ) * TANH_SCALE * (1.0 + 3.0 * CUBIC_TERM * before * before)


def quantize(blocks):
    scales = (jnp.mean(jnp.abs(blocks), axis=-1) + EPSILON).astype(jnp.bfloat16)
    ratios = blocks / scales.astype(jnp.float32)[..., None]
    quants = jnp.clip(ratios, -CLIP_LEVEL, CLIP_LEVEL).astype(jnp.bfloat16)
    return (quants, scales)


def dequantize(quants, scales):
    return quants.astype(jnp.float32) * scales.astype(jnp.float32)[..., None]


def per_device(tokens, weight_q, weight_scale, cotangent):
    node_count = lax.axis_size("node")
    local_count = lax.axis_size("local")
    rows_quant, rows_scale = lax.all_gather((weight_q, weight_scale), "local", axis=0, tiled=True)
    weight = (
        rows_quant.astype(jnp.float32) * jnp.repeat(rows_scale.astype(jnp.float32), BLOCK, axis=1)
    ).astype(jnp.bfloat16)
    before = lax.dot_general(
        tokens, weight, (((1,), (1,)), ((), ())), preferred_element_type=jnp.float32
    )
    activation = gelu_value(before).astype(jnp.bfloat16)
    slope_term = (cotangent.astype(jnp.float32) * gelu_slope(before)).astype(jnp.bfloat16)
    partial_value = lax.dot_general(
        slope_term, tokens, (((0,), (0,)), ((), ())), preferred_element_type=jnp.float32
    )
    blocks = partial_value.reshape(node_count, local_count, -1, BLOCK)
    quant_one, scale_one = quantize(blocks)
    quant_recv = lax.all_to_all(quant_one, "local", split_axis=1, concat_axis=1, tiled=True)
    scale_recv = lax.all_to_all(scale_one, "local", split_axis=1, concat_axis=1, tiled=True)
    group = jnp.sum(dequantize(quant_recv, scale_recv), axis=1)
    quant_two, scale_two = quantize(group)
    quant_recv, scale_recv = (
        lax.all_to_all(quant_two, "node", split_axis=0, concat_axis=0, tiled=True),
        lax.all_to_all(scale_two, "node", split_axis=0, concat_axis=0, tiled=True),
    )
    gradient = jnp.sum(dequantize(quant_recv, scale_recv), axis=0)
    return (activation, gradient)


def solution(mesh):
    return jax.shard_map(
        per_device,
        mesh=mesh,
        in_specs=(
            P(("node", "local"), None),
            P("local", None),
            P("local", None),
            P(("node", "local"), None),
        ),
        out_specs=(P(("node", "local"), None), P(("node", "local"), None)),
        check_vma=False,
    )
```

profile of v0, /device:TPU:1, one launch (start us, length us, event | category | flops | bytes accessed | tf_op | source)
XLA Modules:
  0.0 245.9 jit_solution(14313862257444952505)
XLA Ops:
  7.2 0.0 copy-start
  7.2 0.0 all-gather.4.cloned.1.call-start
  7.2 0.7 all-gather.4.cloned.1.call-update
  7.9 69.0 %all-gather.1 = bf16[32,2,48]{2,1,0:T(2,128)(2,1)S(1)} all-gather(bf16[1,2,48]{2,1,0:T(2,128)(2,1)} %bitcast.18), channel_id=1, replica_groups=mesh['node'=32,'local'=32] {'local'}, dimensions={0}, use_global_device_ids=true | all-gather | bytes 6336 | tf_op jit(solution)/shard_map/all_gather | solution.py:41
  77.0 0.5 broadcast_in_dim.2
  77.4 3.4 %copy.35 = f32[8,8,48,256]{3,1,2,0:T(8,128)} copy(f32[8,8,48,256]{3,2,1,0:T(8,128)S(1)} %bitcast.13) | data formatting | bytes 6291456
  80.9 30.5 %all-gather.4.cloned.1.call-done = bf16[32,2,12288]{2,1,0:T(2,128)(2,1)} async-done(((bf16[1,2,12288]{2,1,0:T(2,128)(2,1)}), bf16[32,2,12288]{2,1,0:T(2,128)(2,1)}) %all-gather.4.cloned.1.call-update) | async-done | bytes 1572880 | tf_op jit(solution)/shard_map/all_gather | solution.py:41
  111.4 4.6 %reshape.57 = f32[64,12288]{1,0:T(8,128)} reshape(bf16[32,2,12288]{2,1,0:T(2,128)(2,1)} %all-gather.4.cloned.1.call-done) | data formatting | bytes 4718592 | tf_op jit(solution)/shard_map/convert_element_type | solution.py:43
  116.0 0.0 copy-done
  116.0 0.0 copy-start.1
  116.0 4.7 %multiply_convert_fusion.4 = (bf16[128,64]{0,1:T(8,128)(2,1)}, f32[128,64]{0,1:T(8,128)S(1)}) fusion(bf16[128,12288]{1,0:T(8,128)(2,1)S(1)} %copy-done, f32[64,12288]{1,0:T(8,128)} %reshape.57, f32[64,12288]{1,0:T(8,128)} %bitcast.14), kind=kOutput, calls=%fused_computation.19 | convolution fusion | flops 202973184 | bytes 9486336 | tf_op jit(solution)/shard_map/dot_general | solution.py:45
  120.7 0.0 copy-done.1
  120.7 2.3 fusion.9
  123.0 5.4 %reshape.51 = f32[32,32,3,256]{3,2,1,0:T(4,128)} reshape(f32[64,12288]{1,0:T(8,128)} %fusion.9) | data formatting | bytes 6291456 | tf_op jit(solution)/shard_map/reshape | solution.py:53
  128.4 4.3 %abs_reduce_fusion = f32[32,32,3]{2,1,0:T(8,128)} fusion(f32[32,32,3,256]{3,2,1,0:T(4,128)} %reshape.51), kind=kLoop, calls=%fused_computation.1 | loop fusion | flops 1569792 | bytes 3158016 | tf_op jit(solution)/shard_map/reduce_sum | solution.py:28
  132.8 1.3 copy.26
  134.1 1.1 copy.27
  135.2 0.7 copy.29
  135.9 6.7 %all-to-all-start.1 = ((bf16[32,32,3]{0,2,1:T(4,128)(2,1)}), bf16[32,32,3]{0,2,1:T(4,128)(2,1)S(1)}, u32[]{:S(2)}, u32[]{:S(2)}) async-start(bf16[32,32,3]{0,2,1:T(4,128)(2,1)} %copy.29), calls=%async_computation.1 | async-start | bytes 65536 | tf_op jit(solution)/shard_map/all_to_all | solution.py:56
  142.6 3.0 %clamp_convert_fusion = bf16[32,32,3,256]{3,2,1,0:T(4,128)(2,1)S(1)} fusion(f32[32,32,3,256]{3,2,1,0:T(4,128)} %reshape.51, f32[32,32,3]{2,1,0:T(8,128)} %copy.27), kind=kLoop, calls=%fused_computation | loop fusion | flops 2359296 | bytes 4730880 | tf_op jit(solution)/shard_map/convert_element_type | solution.py:30
  145.7 2.6 %copy.28 = bf16[32,32,3,256]{3,0,2,1:T(8,128)(2,1)} copy(bf16[32,32,3,256]{3,2,1,0:T(4,128)(2,1)S(1)} %clamp_convert_fusion) | data formatting | bytes 3145728 | tf_op jit(solution)/shard_map/convert_element_type | solution.py:30
  148.3 5.5 %all-to-all-done.1 = bf16[32,32,3]{0,2,1:T(4,128)(2,1)S(1)} async-done(((bf16[32,32,3]{0,2,1:T(4,128)(2,1)}), bf16[32,32,3]{0,2,1:T(4,128)(2,1)S(1)}, u32[]{:S(2)}, u32[]{:S(2)}) %all-to-all-start.1) | async-done | bytes 6176 | tf_op jit(solution)/shard_map/all_to_all | solution.py:56
  153.7 6.3 %all-to-all-start = ((bf16[32,32,3,256]{3,0,2,1:T(8,128)(2,1)}), bf16[32,32,3,256]{3,0,2,1:T(8,128)(2,1)}, u32[]{:S(2)}, u32[]{:S(2)}) async-start(bf16[32,32,3,256]{3,0,2,1:T(8,128)(2,1)} %copy.28), calls=%async_computation | async-start | bytes 3145728 | tf_op jit(solution)/shard_map/all_to_all | solution.py:55
  160.0 38.7 %all-to-all-done = bf16[32,32,3,256]{3,0,2,1:T(8,128)(2,1)} async-done(((bf16[32,32,3,256]{3,0,2,1:T(8,128)(2,1)}), bf16[32,32,3,256]{3,0,2,1:T(8,128)(2,1)}, u32[]{:S(2)}, u32[]{:S(2)}) %all-to-all-start) | async-done | bytes 1572896 | tf_op jit(solution)/shard_map/all_to_all | solution.py:55
  198.8 1.9 multiply_reduce_fusion
  200.6 0.1 abs_reduce_fusion.1
  200.7 0.7 copy.31
  201.5 16.8 %all-to-all-start.3 = ((bf16[32,1,3]{2,1,0:T(2,128)(2,1)}), bf16[32,1,3]{2,1,0:T(2,128)(2,1)S(1)}, u32[]{:S(2)}, u32[]{:S(2)}) async-start(bf16[32,1,3]{2,1,0:T(2,128)(2,1)} %copy.31), calls=%async_computation.3 | async-start | bytes 32768 | tf_op jit(solution)/shard_map/all_to_all | solution.py:61
  218.2 0.1 clamp_convert_fusion.1
  218.3 0.7 copy.30
  219.0 7.1 %all-to-all-done.3 = bf16[32,1,3]{2,1,0:T(2,128)(2,1)S(1)} async-done(((bf16[32,1,3]{2,1,0:T(2,128)(2,1)}), bf16[32,1,3]{2,1,0:T(2,128)(2,1)S(1)}, u32[]{:S(2)}, u32[]{:S(2)}) %all-to-all-start.3) | async-done | bytes 224 | tf_op jit(solution)/shard_map/all_to_all | solution.py:61
  226.1 4.2 %all-to-all-start.2 = ((bf16[32,3,256]{2,1,0:T(4,128)(2,1)}), bf16[32,3,256]{2,1,0:T(4,128)(2,1)S(1)}, u32[]{:S(2)}, u32[]{:S(2)}) async-start(bf16[32,3,256]{2,1,0:T(4,128)(2,1)} %copy.30), calls=%async_computation.2 | async-start | bytes 131072 | tf_op jit(solution)/shard_map/all_to_all | solution.py:60
  230.3 0.1 copy.32
  230.4 0.1 copy.34
  230.5 7.8 %all-to-all-done.2 = bf16[32,3,256]{2,1,0:T(4,128)(2,1)S(1)} async-done(((bf16[32,3,256]{2,1,0:T(4,128)(2,1)}), bf16[32,3,256]{2,1,0:T(4,128)(2,1)S(1)}, u32[]{:S(2)}, u32[]{:S(2)}) %all-to-all-start.2) | async-done | bytes 49184 | tf_op jit(solution)/shard_map/all_to_all | solution.py:60
  238.3 0.7 multiply_reduce_fusion.1
  (3 shorter events, 0.0 us)
Async XLA Ops:
  7.2 108.9 %copy-start = (bf16[128,12288]{1,0:T(8,128)(2,1)S(1)}, bf16[128,12288]{1,0:T(8,128)(2,1)}, u32[]{:S(2)}) copy-start(bf16[128,12288]{1,0:T(8,128)(2,1)} %param.4) | copy-start | bytes 9437188
  7.2 104.2 %all-gather.4.cloned.1.call-start = ((), (), s32[]{:S(2)}) async-start(), calls=%async_computation.4 | async-start | bytes 1622016 | tf_op jit(solution)/shard_map/all_gather | solution.py:41
  116.0 4.7 %copy-start.1 = (bf16[128,64]{0,1:T(8,128)(2,1)S(1)}, bf16[128,64]{0,1:T(8,128)(2,1)}, u32[]{:S(2)}) copy-start(bf16[128,64]{0,1:T(8,128)(2,1)} %param.7) | copy-start | bytes 49156
  135.9 17.9 %all-to-all-start.1 = ((bf16[32,32,3]{0,2,1:T(4,128)(2,1)}), bf16[32,32,3]{0,2,1:T(4,128)(2,1)S(1)}, u32[]{:S(2)}, u32[]{:S(2)}) async-start(bf16[32,32,3]{0,2,1:T(4,128)(2,1)} %copy.29), calls=%async_computation.1 | async-start | bytes 65536 | tf_op jit(solution)/shard_map/all_to_all | solution.py:56
  153.7 45.0 %all-to-all-start = ((bf16[32,32,3,256]{3,0,2,1:T(8,128)(2,1)}), bf16[32,32,3,256]{3,0,2,1:T(8,128)(2,1)}, u32[]{:S(2)}, u32[]{:S(2)}) async-start(bf16[32,32,3,256]{3,0,2,1:T(8,128)(2,1)} %copy.28), calls=%async_computation | async-start | bytes 3145728 | tf_op jit(solution)/shard_map/all_to_all | solution.py:55
  201.5 24.6 %all-to-all-start.3 = ((bf16[32,1,3]{2,1,0:T(2,128)(2,1)}), bf16[32,1,3]{2,1,0:T(2,128)(2,1)S(1)}, u32[]{:S(2)}, u32[]{:S(2)}) async-start(bf16[32,1,3]{2,1,0:T(2,128)(2,1)} %copy.31), calls=%async_computation.3 | async-start | bytes 32768 | tf_op jit(solution)/shard_map/all_to_all | solution.py:61
  226.1 12.3 %all-to-all-start.2 = ((bf16[32,3,256]{2,1,0:T(4,128)(2,1)}), bf16[32,3,256]{2,1,0:T(4,128)(2,1)S(1)}, u32[]{:S(2)}, u32[]{:S(2)}) async-start(bf16[32,3,256]{2,1,0:T(4,128)(2,1)} %copy.30), calls=%async_computation.2 | async-start | bytes 131072 | tf_op jit(solution)/shard_map/all_to_all | solution.py:60
Sparse Core Ops, SparseCore 0:
  12.4 99.0 all-gather.3
where the time goes:
time: 246 us
  waiting for transfers between devices  90.3 us (37%)
  blocking collectives  69 us (28%)
  starting transfers between devices  34.1 us (14%)
  local copies, waits for them, and re-layouts  21.2 us (9%)
  between operations  14.1 us (6%)
  other arithmetic  10.2 us (4%)
  matrix products  6.95 us (3%)
    all_gather x1, blocking collectives, per_device(): lax.all_gather((weight_q, weight_scale), 'local', axis=0, tiled=True)  69 us
    all_to_all x1, waiting for transfers between devices, per_device(): lax.all_to_all(quant_one, 'local', split_axis=1, concat_axis=1, tiled=True)  38.7 us
    all_gather x1, waiting for transfers between devices, per_device(): lax.all_gather((weight_q, weight_scale), 'local', axis=0, tiled=True)  30.5 us
    all_to_all x1, starting transfers between devices, per_device(): lax.all_to_all(scale_two, 'node', split_axis=0, concat_axis=0, tiled=True)  16.8 us
    all_to_all x1, waiting for transfers between devices, per_device(): lax.all_to_all(quant_two, 'node', split_axis=0, concat_axis=0, tiled=True)  7.84 us
    all_to_all x1, waiting for transfers between devices, per_device(): lax.all_to_all(scale_two, 'node', split_axis=0, concat_axis=0, tiled=True)  7.07 us
    all_to_all x1, starting transfers between devices, per_device(): lax.all_to_all(scale_one, 'local', split_axis=1, concat_axis=1, tiled=True)  6.75 us
    all_to_all x1, starting transfers between devices, per_device(): lax.all_to_all(quant_one, 'local', split_axis=1, concat_axis=1, tiled=True)  6.26 us
  transfers between devices with their start and end apart: 5, of which 5 were waited for; matrix products, arithmetic and copies ran while one was open for 4% of the time, Pallas kernels for 0%

commit v1 on v0

v1 whole, which is shorter than its diff:
```python
import jax
import jax.numpy as jnp
from jax import lax
from jax.experimental import pallas as pl
from jax.experimental.pallas import tpu as pltpu
from jax.sharding import PartitionSpec as P

BLOCK = 256
EPSILON = 1e-06
CLIP_LEVEL = 3.0
TANH_SCALE = 0.7978845608028654
CUBIC_TERM = 0.044715
SUB = 16
VMEM_LIMIT = 48 * 1024 * 1024


def clip_blocks(values):
    parts = []
    for k in range(values.shape[1] // BLOCK):
        block = values[:, k * BLOCK : (k + 1) * BLOCK]
        mean = jnp.sum(jnp.abs(block), axis=1, keepdims=True) * (1.0 / BLOCK)
        scale = (mean + EPSILON).astype(jnp.bfloat16).astype(jnp.float32)
        bound = CLIP_LEVEL * scale
        parts.append(jnp.minimum(jnp.maximum(block, -bound), bound))
    return jnp.concatenate(parts, axis=1)


def gradient_kernel(half_ref, tokens_ref, own_ref, other_ref, cot_ref, act_ref, out_ref):
    width = own_ref.shape[2]
    rows = own_ref.shape[0] * SUB
    cols = SUB // 2
    batch = tokens_ref.shape[0]
    which = lax.broadcasted_iota(jnp.int32, (rows, 1), 0) % cols
    total = jnp.zeros((rows, batch), jnp.float32)
    for part, ref in enumerate((own_ref, other_ref)):
        start = (half_ref[0] if part == 0 else 1 - half_ref[0]) * (cols * width)
        weight = ref[...].reshape(rows, width)
        for c in range(cols):
            columns = pl.ds(pl.multiple_of(start + c * width, 128), width)
            product = lax.dot_general(
                weight, tokens_ref[:, columns], (((1,), (1,)), ((), ())), preferred_element_type=jnp.float32
            )
            total = total + jnp.where(which == c, product, 0.0)
    before = jnp.sum(total.reshape(rows // cols, cols, batch), axis=1)

    tanh_inner = jnp.tanh(TANH_SCALE * (before + CUBIC_TERM * before * before * before))
    act = 0.5 * before * (1.0 + tanh_inner)
    act_ref[...] = act.T.astype(jnp.bfloat16)
    slope = 0.5 * (1.0 + tanh_inner) + 0.5 * before * (1.0 - tanh_inner * tanh_inner) * TANH_SCALE * (
        1.0 + 3.0 * CUBIC_TERM * before * before
    )
    slope = (cot_ref[...].astype(jnp.float32).T * slope).astype(jnp.bfloat16)
    hidden = slope.shape[0]
    to = lax.broadcasted_iota(jnp.int32, (hidden, hidden), 0)
    source = lax.broadcasted_iota(jnp.int32, (hidden, hidden), 1)
    pick = source == (to % (hidden // 2)) * 2 + to // (hidden // 2)
    slope = jnp.dot(
        jnp.where(pick, 1.0, 0.0).astype(jnp.bfloat16), slope, preferred_element_type=jnp.float32
    ).astype(jnp.bfloat16)

    slots, nodes, piece = out_ref.shape
    for i in range(slots // 2):
        partial = jnp.dot(slope, tokens_ref[:, i * piece : (i + 1) * piece], preferred_element_type=jnp.float32)
        value = clip_blocks(partial).astype(jnp.bfloat16)
        out_ref[i] = value[:nodes]
        out_ref[slots // 2 + i] = value[nodes:]


def group_kernel(parts_ref, out_ref):
    total = parts_ref[0].astype(jnp.float32)
    for i in range(1, parts_ref.shape[0]):
        total = total + parts_ref[i].astype(jnp.float32)
    out_ref[...] = clip_blocks(total).astype(jnp.bfloat16)


def per_device(tokens, weight_q, weight_scale, cotangent):
    node_count = lax.axis_size("node")
    local_count = lax.axis_size("local")
    batch, depth = tokens.shape
    own_rows = weight_q.shape[0]
    hidden = cotangent.shape[1]
    half = lax.axis_index("node") % 2
    piece = hidden * depth // (node_count * local_count)

    weight = (
        weight_q.astype(jnp.float32) * jnp.repeat(weight_scale.astype(jnp.float32), BLOCK, axis=1)
    ).astype(jnp.bfloat16)
    mine = lax.dynamic_slice_in_dim(weight, half * (depth // 2), depth // 2, axis=1)
    mine = mine.reshape(SUB, own_rows * depth // 2 // SUB)
    copies = jnp.broadcast_to(mine[None], (local_count,) + mine.shape)
    own = lax.all_to_all(copies, "local", split_axis=0, concat_axis=0, tiled=True)
    other = lax.ppermute(own, "node", [(n, n ^ 1) for n in range(node_count)])

    vmem = pl.BlockSpec(memory_space=pltpu.VMEM)
    activation, sent = pl.pallas_call(
        gradient_kernel,
        out_shape=(
            jax.ShapeDtypeStruct((batch, hidden), jnp.bfloat16),
            jax.ShapeDtypeStruct((local_count, node_count, piece), jnp.bfloat16),
        ),
        in_specs=[pl.BlockSpec(memory_space=pltpu.SMEM)] + [vmem] * 4,
        out_specs=(vmem, vmem),
        compiler_params=pltpu.CompilerParams(vmem_limit_bytes=VMEM_LIMIT),
    )(half.astype(jnp.int32).reshape(1), tokens, own, other, cotangent)

    got = lax.all_to_all(sent, "local", split_axis=0, concat_axis=0, tiled=True)
    group = pl.pallas_call(
        group_kernel,
        out_shape=jax.ShapeDtypeStruct((node_count, piece), jnp.bfloat16),
        in_specs=[vmem],
        out_specs=vmem,
        compiler_params=pltpu.CompilerParams(vmem_limit_bytes=VMEM_LIMIT),
    )(got)
    group = group.reshape(node_count, piece // BLOCK, BLOCK)
    got = lax.all_to_all(group, "node", split_axis=0, concat_axis=0, tiled=True)
    gradient = jnp.sum(got.astype(jnp.float32), axis=0)
    return (activation, gradient)


def solution(mesh):
    return jax.shard_map(
        per_device,
        mesh=mesh,
        in_specs=(
            P(("node", "local"), None),
            P("local", None),
            P("local", None),
            P(("node", "local"), None),
        ),
        out_specs=(P(("node", "local"), None), P(("node", "local"), None)),
        check_vma=False,
    )
```

time: 246 us -> 128 us (0.52)
  waiting for transfers between devices: 90.3 us -> 9 us
  local copies, waits for them, and re-layouts: 21.2 us -> 1.69 us
  between operations: 14.1 us -> 0.72 us
  blocking collectives: 69 us -> 78.1 us
  other arithmetic: 10.2 us -> 2.07 us
  Pallas kernels: 0 us -> 6.96 us
  matrix products: 6.95 us -> 0 us
  starting transfers between devices: 34.1 us -> 28.4 us
    all_to_all x0 -> x2, blocking collectives: none -> 78.1 us  [the longest x1 45.6 us: per_device(): got = lax.all_to_all(sent, 'local', split_axis=0, concat_axis=0, tiled=True)]
    all_gather x1 -> x0, blocking collectives: 69 us -> none  [per_device(): lax.all_gather((weight_q, weight_scale), 'local', axis=0, tiled=True)]
    all_to_all x4 -> x1, waiting for transfers between devices: 59.1 us -> 7.23 us  [per_device(): got = lax.all_to_all(group, 'node', split_axis=0, concat_axis=0, tiled=True)]
    all_gather x1 -> x0, waiting for transfers between devices: 30.5 us -> none  [per_device(): lax.all_gather((weight_q, weight_scale), 'local', axis=0, tiled=True)]
    all_to_all x4 -> x1, starting transfers between devices: 34 us -> 20.5 us  [per_device(): got = lax.all_to_all(group, 'node', split_axis=0, concat_axis=0, tiled=True)]
    convert_element_type x7 -> x0, local copies, waits for them, and re-layouts: 10.4 us -> none  [the longest x1 4.62 us: per_device(): rows_quant.astype(jnp.float32)]
    ppermute x0 -> x1, starting transfers between devices: none -> 7.88 us  [per_device(): other = lax.ppermute(own, 'node', [(n, n ^ 1) for n in range(node_count)])]
    pallas_call x0 -> x2, Pallas kernels: none -> 6.96 us  [the longest x1 6.66 us: per_device(): pl.pallas_call(gradient_kernel, out_shape=(jax.ShapeDtypeStruct((batch, h...]
  transfers between devices with their start and end apart: 5 -> 2, of which waited for: 5 -> 2; matrix products, arithmetic and copies ran while one was open for 4% -> 1% of each run, Pallas kernels for 0% -> 0%
where the time goes in v1:
time: 128 us; the launch traced here: 127 us
  blocking collectives  78.1 us (61%)
  starting transfers between devices  28.4 us (22%)
  waiting for transfers between devices  9 us (7%)
  Pallas kernels  6.96 us (5%)
  other arithmetic  2.07 us (2%)
  local copies, waits for them, and re-layouts  1.69 us (1%)
    all_to_all x1, blocking collectives, per_device(): got = lax.all_to_all(sent, 'local', split_axis=0, concat_axis=0, tiled=True)  45.6 us
    all_to_all x1, blocking collectives, per_device(): lax.all_to_all(copies, 'local', split_axis=0, concat_axis=0, tiled=True)  32.5 us
    all_to_all x1, starting transfers between devices, per_device(): got = lax.all_to_all(group, 'node', split_axis=0, concat_axis=0, tiled=True)  20.5 us
    ppermute x1, starting transfers between devices, per_device(): other = lax.ppermute(own, 'node', [(n, n ^ 1) for n in range(node_count)])  7.88 us
    all_to_all x1, waiting for transfers between devices, per_device(): got = lax.all_to_all(group, 'node', split_axis=0, concat_axis=0, tiled=True)  7.23 us
    pallas_call x1, Pallas kernels, per_device(): pl.pallas_call(gradient_kernel, out_shape=(jax.ShapeDtypeStruct((batch, h...  6.66 us
  transfers between devices with their start and end apart: 2, of which 2 were waited for; matrix products, arithmetic and copies ran while one was open for 1% of the time, Pallas kernels for 0%

profile of v1, /device:TPU:1, one launch (start us, length us, event | category | flops | bytes accessed | tf_op | source)
XLA Modules:
  0.0 126.9 jit_solution(16520735345309287120)
XLA Ops:
  0.6 0.0 copy-start
  0.7 0.7 convert_element_type.13
  1.3 0.1 broadcast_bitcast_fusion
  1.4 0.1 copy.10
  1.5 0.8 fusion
  2.3 0.1 broadcast_in_dim.12
  2.3 32.5 %all_to_all.15.own_ref = bf16[32,16,768]{2,1,0:T(8,128)(2,1)S(1)} all-to-all(bf16[32,16,768]{2,1,0:T(8,128)(2,1)S(1)} %broadcast_in_dim.12), channel_id=1, replica_groups=mesh['node'=32,'local'=32] {'local'}, dimensions={0} | all-to-all | bytes 1572864 | tf_op jit(solution)/shard_map/all_to_all | solution.py:91
  34.8 7.9 %collective-permute-start = (bf16[32,16,768]{2,1,0:T(8,128)(2,1)S(1)}, bf16[32,16,768]{2,1,0:T(8,128)(2,1)S(1)}, u32[]{:S(2)}, u32[]{:S(2)}) collective-permute-start(bf16[32,16,768]{2,1,0:T(8,128)(2,1)S(1)} %all_to_all.15.own_ref), channel_id=1, source_target_pairs={{0,32},{32,0},{64,96},{96,64},{128,160},{160,128},{192,224},{224,1... | collective-permute-start | bytes 2359304 | tf_op jit(solution)/shard_map/ppermute | solution.py:92
  42.7 0.0 copy-done
  42.7 0.1 copy.8.cot_ref
  42.9 1.8 %collective-permute-done.other_ref = bf16[32,16,768]{2,1,0:T(8,128)(2,1)S(1)} collective-permute-done((bf16[32,16,768]{2,1,0:T(8,128)(2,1)S(1)}, bf16[32,16,768]{2,1,0:T(8,128)(2,1)S(1)}, u32[]{:S(2)}, u32[]{:S(2)}) %collective-permute-start) | collective-permute-done | bytes 786464 | tf_op jit(solution)/shard_map/ppermute | solution.py:92
  44.6 6.7 %shard_map.59 = (bf16[128,64]{1,0:T(8,128)(2,1)S(1)}, bf16[32,32,768]{2,1,0:T(8,128)(2,1)S(1)}) custom-call(s32[1]{0:T(128)} %bitcast.half_ref, bf16[128,12288]{1,0:T(8,128)(2,1)} %tokens_ref.1, bf16[32,16,768]{2,1,0:T(8,128)(2,1)S(1)} %all_to_all.15.own_ref, bf16[32,16,768]{2,1,0:T(8,128)(2,1)S(1)} %collective-permute-done.other_ref, ...), custom_call_target="tpu_custom_call" | custom-call | tf_op jit(solution)/shard_map/pallas_call | solution.py:95
  51.3 45.6 %all_to_all.16.parts_ref = bf16[32,32,768]{2,1,0:T(8,128)(2,1)S(1)} all-to-all(bf16[32,32,768]{2,1,0:T(8,128)(2,1)S(1)} %get-tuple-element.5), channel_id=1, replica_groups=mesh['node'=32,'local'=32] {'local'}, dimensions={0} | all-to-all | bytes 3145728 | tf_op jit(solution)/shard_map/all_to_all | solution.py:106
  96.9 0.3 shard_map.60
  97.2 0.6 reshape.16
  97.8 20.5 %all-to-all-start.2 = ((bf16[32,3,256]{2,1,0:T(4,128)(2,1)}), bf16[32,3,256]{2,1,0:T(4,128)(2,1)S(1)}, u32[]{:S(2)}, u32[]{:S(2)}) async-start(bf16[32,3,256]{2,1,0:T(4,128)(2,1)} %reshape.16), calls=%async_computation.2 | async-start | bytes 131072 | tf_op jit(solution)/shard_map/all_to_all | solution.py:115
  118.3 0.7 copy.9
  119.0 7.2 %all-to-all-done.2 = bf16[32,3,256]{2,1,0:T(4,128)(2,1)S(1)} async-done(((bf16[32,3,256]{2,1,0:T(4,128)(2,1)}), bf16[32,3,256]{2,1,0:T(4,128)(2,1)S(1)}, u32[]{:S(2)}, u32[]{:S(2)}) %all-to-all-start.2) | async-done | bytes 49184 | tf_op jit(solution)/shard_map/all_to_all | solution.py:115
  126.3 0.6 convert_reduce_fusion
  (1 shorter events, 0.0 us)
Async XLA Ops:
  0.6 42.1 %copy-start = (bf16[128,64]{0,1:T(8,128)(2,1)S(1)}, bf16[128,64]{0,1:T(8,128)(2,1)}, u32[]{:S(2)}) copy-start(bf16[128,64]{0,1:T(8,128)(2,1)} %param.7) | copy-start | bytes 49156
  34.8 9.8 %collective-permute-start = (bf16[32,16,768]{2,1,0:T(8,128)(2,1)S(1)}, bf16[32,16,768]{2,1,0:T(8,128)(2,1)S(1)}, u32[]{:S(2)}, u32[]{:S(2)}) collective-permute-start(bf16[32,16,768]{2,1,0:T(8,128)(2,1)S(1)} %all_to_all.15.own_ref), channel_id=1, source_target_pairs={{0,32},{32,0},{64,96},{96,64},{128,160},{160,128},{192,224},{224,1... | collective-permute-start | bytes 2359304 | tf_op jit(solution)/shard_map/ppermute | solution.py:92
  97.8 28.4 %all-to-all-start.2 = ((bf16[32,3,256]{2,1,0:T(4,128)(2,1)}), bf16[32,3,256]{2,1,0:T(4,128)(2,1)S(1)}, u32[]{:S(2)}, u32[]{:S(2)}) async-start(bf16[32,3,256]{2,1,0:T(4,128)(2,1)} %reshape.16), calls=%async_computation.2 | async-start | bytes 131072 | tf_op jit(solution)/shard_map/all_to_all | solution.py:115

commit v2 on v0

v2 whole, which is shorter than its diff:
```python
import functools

import jax
import jax.numpy as jnp
from jax import lax
from jax.experimental import pallas as pl
from jax.experimental.pallas import tpu as pltpu
from jax.sharding import Mesh, PartitionSpec as P

BLOCK = 256
EPSILON = 1e-06
CLIP_LEVEL = 3.0
TANH_SCALE = 0.7978845608028654
CUBIC_TERM = 0.044715
ROWS = 16
RING_Y, RING_X = 4, 8
PARAMS = pltpu.CompilerParams(vmem_limit_bytes=24 * 1024 * 1024)
VMEM = pl.BlockSpec(memory_space=pltpu.VMEM)
SMEM = pl.BlockSpec(memory_space=pltpu.SMEM)


def shape(dims, dtype=jnp.bfloat16):
    return jax.ShapeDtypeStruct(dims, dtype)


def clip_block(block):
    mean = jnp.sum(jnp.abs(block), axis=1, keepdims=True) * (1.0 / BLOCK)
    scale = (mean + EPSILON).astype(jnp.bfloat16).astype(jnp.float32)
    bound = CLIP_LEVEL * scale
    return jnp.minimum(jnp.maximum(block, -bound), bound).astype(jnp.bfloat16)


def clip_blocks(values):
    return jnp.concatenate(
        [clip_block(values[:, k : k + BLOCK]) for k in range(0, values.shape[1], BLOCK)], axis=1
    )


def weight_kernel(half_ref, quant_ref, scale_ref, out_ref):
    own_rows, depth = quant_ref.shape
    width = out_ref.shape[2]
    pieces = depth // 2 // width
    first = half_ref[0] == 0
    scales = scale_ref[...].astype(jnp.float32)
    rows = []
    for r in range(own_rows):
        for c in range(pieces):
            halves = []
            for start in (c * width, depth // 2 + c * width):
                quant = quant_ref[r : r + 1, start : start + width].astype(jnp.float32)
                spread = [
                    jnp.broadcast_to(scales[r : r + 1, k : k + 1], (1, BLOCK))
                    for k in range(start // BLOCK, (start + width) // BLOCK)
                ]
                halves.append(quant * jnp.concatenate(spread, axis=1))
            rows.append(jnp.where(first, halves[0], halves[1]))
    weight = jnp.concatenate(rows, axis=0).astype(jnp.bfloat16)
    for slot in range(out_ref.shape[0]):
        out_ref[slot] = weight


def before_half(half, tokens_ref, rows_ref):
    batch = tokens_ref.shape[0]
    count, width = rows_ref.shape[0] * ROWS, rows_ref.shape[2]
    pieces = ROWS // 2
    weight = rows_ref[...].reshape(count, width)
    which = lax.broadcasted_iota(jnp.int32, (count, 1), 0) % pieces
    total = jnp.zeros((count, batch), jnp.float32)
    for c in range(0, pieces, 2):
        pair = [
            tokens_ref[:, pl.ds(pl.multiple_of((half * pieces + c + k) * width, 128), width)] for k in range(2)
        ]
        product = lax.dot_general(
            weight, jnp.concatenate(pair, axis=0), (((1,), (1,)), ((), ())), preferred_element_type=jnp.float32
        )
        total = total + jnp.where(which == c, product[:, :batch], 0.0)
        total = total + jnp.where(which == c + 1, product[:, batch:], 0.0)
    return jnp.sum(total.reshape(count // pieces, pieces, batch), axis=1)


def own_kernel(half_ref, tokens_ref, rows_ref, out_ref):
    out_ref[...] = before_half(half_ref[0], tokens_ref, rows_ref)


def first_kernel(half_ref, tokens_ref, rows_ref, own_ref, cot_ref, act_ref, sent_ref):
    before = own_ref[...] + before_half(1 - half_ref[0], tokens_ref, rows_ref)
    tanh_inner = jnp.tanh(TANH_SCALE * (before + CUBIC_TERM * before * before * before))
    act_ref[...] = (0.5 * before * (1.0 + tanh_inner)).astype(jnp.bfloat16)
    slope = 0.5 * (1.0 + tanh_inner) + 0.5 * before * (1.0 - tanh_inner * tanh_inner) * TANH_SCALE * (
        1.0 + 3.0 * CUBIC_TERM * before * before
    )
    slope = (cot_ref[...].astype(jnp.float32) * slope).astype(jnp.bfloat16)
    hidden = slope.shape[0]
    to = lax.broadcasted_iota(jnp.int32, (hidden, hidden), 0)
    source = lax.broadcasted_iota(jnp.int32, (hidden, hidden), 1)
    pick = source == to % (hidden // 2) * 2 + to // (hidden // 2)
    slope = jnp.dot(
        jnp.where(pick, 1.0, 0.0).astype(jnp.bfloat16), slope, preferred_element_type=jnp.float32
    ).astype(jnp.bfloat16)
    nodes = slope.shape[0] // 2
    per_row = RING_Y * RING_X // 2
    piece = tokens_ref.shape[1] // per_row
    for i in range(per_row):
        partial = jnp.dot(slope, tokens_ref[:, i * piece : (i + 1) * piece], preferred_element_type=jnp.float32)
        value = clip_blocks(partial)
        for row_parity in range(2):
            owner = row_parity * per_row + i
            sent_ref[owner] = value[row_parity * nodes : (row_parity + 1) * nodes]


def group_kernel(got_ref, out_ref):
    total = got_ref[0].astype(jnp.float32)
    for i in range(1, got_ref.shape[0]):
        total = total + got_ref[i].astype(jnp.float32)
    for k in range(out_ref.shape[1]):
        out_ref[:, k, :] = clip_block(total[:, k * BLOCK : (k + 1) * BLOCK])


def per_device(tokens, weight_q, weight_scale, cotangent):
    node_count = lax.axis_size("node")
    local_count = RING_Y * RING_X
    batch, depth = tokens.shape
    own_rows = weight_q.shape[0]
    hidden = cotangent.shape[1]
    piece = hidden * depth // (node_count * local_count)
    side = node_count // 2
    half = (lax.axis_index("node") % 2).astype(jnp.int32).reshape(1)
    parity = lax.axis_index("parity").astype(jnp.int32).reshape(1)
    call = functools.partial(pl.pallas_call, compiler_params=PARAMS)

    share = shape((local_count, ROWS, own_rows * depth // 2 // ROWS))
    copies = call(weight_kernel, out_shape=share, in_specs=[SMEM, VMEM, VMEM], out_specs=VMEM)(
        half, weight_q, weight_scale
    )
    own = lax.all_to_all(copies, ("y", "pair", "parity"), split_axis=0, concat_axis=0, tiled=True)
    other = lax.ppermute(own, "node", [(n, n ^ 1) for n in range(node_count)])
    before = call(
        own_kernel, out_shape=shape((hidden, batch), jnp.float32), in_specs=[SMEM, VMEM, VMEM], out_specs=VMEM
    )(half, tokens, own)
    activation, sent = call(
        first_kernel,
        out_shape=(shape((hidden, batch)), shape((local_count, node_count, piece))),
        in_specs=[SMEM] + [VMEM] * 4,
        out_specs=(VMEM,) * 2,
    )(half, tokens, other, before, cotangent.T)
    got = lax.all_to_all(sent, ("y", "pair", "parity"), split_axis=0, concat_axis=0, tiled=True)
    group = call(
        group_kernel, out_shape=shape((node_count, piece // BLOCK, BLOCK)), in_specs=[VMEM], out_specs=VMEM
    )(got)
    got = lax.all_to_all(group, "node", split_axis=0, concat_axis=0, tiled=True)
    gradient = jnp.sum(got.astype(jnp.float32), axis=0)
    return (activation.T, gradient)


def solution(mesh):
    axes = ("node", "y", "pair", "parity")
    fine = Mesh(mesh.devices.reshape(mesh.devices.shape[0], RING_Y, RING_X // 2, 2), axes)
    everywhere, group = P(axes, None), P(axes[1:], None)
    return jax.shard_map(
        per_device,
        mesh=fine,
        in_specs=(everywhere, group, group, everywhere),
        out_specs=(everywhere, everywhere),
        check_vma=False,
    )
```

time: 246 us -> 124 us (0.50)
  waiting for transfers between devices: 90.3 us -> 0.01 us
  blocking collectives: 69 us -> 107 us
  starting transfers between devices: 34.1 us -> 7.88 us
  local copies, waits for them, and re-layouts: 21.2 us -> 3.33 us
  between operations: 14.1 us -> 0.71 us
  other arithmetic: 10.2 us -> 0.64 us
  matrix products: 6.95 us -> 0 us
  Pallas kernels: 0 us -> 3.88 us
    all_to_all x0 -> x3, blocking collectives: none -> 107 us  [the longest x1 46 us: per_device(): lax.all_to_all(sent, ('y', 'pair', 'parity'), split_axis=0, concat_axis=0...]
    all_gather x1 -> x0, blocking collectives: 69 us -> none  [per_device(): lax.all_gather((weight_q, weight_scale), 'local', axis=0, tiled=True)]
    all_to_all x4 -> x0, waiting for transfers between devices: 59.1 us -> none  [the longest x1 38.7 us: per_device(): lax.all_to_all(quant_one, 'local', split_axis=1, concat_axis=1, tiled=True)]
    all_to_all x4 -> x0, starting transfers between devices: 34 us -> none  [the longest x1 16.8 us: per_device(): lax.all_to_all(scale_two, 'node', split_axis=0, concat_axis=0, tiled=True)]
    all_gather x1 -> x0, waiting for transfers between devices: 30.5 us -> none  [per_device(): lax.all_gather((weight_q, weight_scale), 'local', axis=0, tiled=True)]
    convert_element_type x7 -> x0, local copies, waits for them, and re-layouts: 10.4 us -> none  [the longest x1 4.62 us: per_device(): rows_quant.astype(jnp.float32)]
    ppermute x0 -> x1, starting transfers between devices: none -> 7.88 us  [per_device(): other = lax.ppermute(own, 'node', [(n, n ^ 1) for n in range(node_count)])]
    dot_general x2 -> x0, matrix products: 6.95 us -> none  [the longest x1 4.68 us: per_device(): lax.dot_general(tokens, weight, (((1,), (1,)), ((), ())), preferred_eleme...]
  transfers between devices with their start and end apart: 5 -> 1, of which waited for: 5 -> 0; matrix products, arithmetic and copies ran while one was open for 4% -> 0% of each run, Pallas kernels for 0% -> 1%
where the time goes in v2:
time: 124 us; the launch traced here: 123 us
  blocking collectives  107 us (86%)
  starting transfers between devices  7.88 us (6%)
  Pallas kernels  3.88 us (3%)
  local copies, waits for them, and re-layouts  3.33 us (3%)
    all_to_all x1, blocking collectives, per_device(): lax.all_to_all(sent, ('y', 'pair', 'parity'), split_axis=0, concat_axis=0...  46 us
    all_to_all x1, blocking collectives, per_device(): lax.all_to_all(copies, ('y', 'pair', 'parity'), split_axis=0, concat_axis...  32.5 us
    all_to_all x1, blocking collectives, per_device(): got = lax.all_to_all(group, 'node', split_axis=0, concat_axis=0, tiled=True)  28.3 us
    ppermute x1, starting transfers between devices, per_device(): other = lax.ppermute(own, 'node', [(n, n ^ 1) for n in range(node_count)])  7.88 us
    unnamed x8, local copies, waits for them, and re-layouts  3.33 us
  transfers between devices with their start and end apart: 1, of which 0 were waited for; matrix products, arithmetic and copies ran while one was open for 0% of the time, Pallas kernels for 1%

profile of v2, /device:TPU:1, one launch (start us, length us, event | category | flops | bytes accessed | tf_op | source)
XLA Modules:
  0.0 123.3 jit_solution(8074795466348199632)
XLA Ops:
  0.6 0.0 copy-start.1
  0.7 0.8 copy-done.1
  1.4 0.0 copy-start.3
  1.4 0.7 copy-done.3
  2.1 0.2 shard_map.59
  2.3 32.5 %all_to_all.15.rows_ref = bf16[32,16,768]{2,1,0:T(8,128)(2,1)S(1)} all-to-all(bf16[32,16,768]{2,1,0:T(8,128)(2,1)S(1)} %shard_map.59), channel_id=1, replica_groups=mesh['node'=32,'y'=4,'pair'=4,'parity'=2] {'y','pair','parity'}, dimensions={0} | all-to-all | bytes 1572864 | tf_op jit(solution)/shard_map/all_to_all | solution.py:135
  34.8 7.9 %collective-permute-start = (bf16[32,16,768]{2,1,0:T(8,128)(2,1)S(1)}, bf16[32,16,768]{2,1,0:T(8,128)(2,1)S(1)}, u32[]{:S(2)}, u32[]{:S(2)}) collective-permute-start(bf16[32,16,768]{2,1,0:T(8,128)(2,1)S(1)} %all_to_all.15.rows_ref), channel_id=1, source_target_pairs={{0,32},{32,0},{64,96},{96,64},{128,160},{160,128},{192,224},{224,1... | collective-permute-start | bytes 2359304 | tf_op jit(solution)/shard_map/ppermute | solution.py:136
  42.7 0.0 copy-start
  42.7 1.9 %copy-done = bf16[128,12288]{1,0:T(8,128)(2,1)S(1)} copy-done((bf16[128,12288]{1,0:T(8,128)(2,1)S(1)}, bf16[128,12288]{1,0:T(8,128)(2,1)}, u32[]{:S(2)}) %copy-start) | copy-done | bytes 3145752
  44.6 0.0 copy-start.2
  44.6 1.1 shard_map.60.own_ref
  45.6 0.0 collective-permute-done.rows_ref
  45.7 0.0 copy-done.2
  45.7 2.3 %shard_map.61 = (bf16[64,128]{1,0:T(8,128)(2,1)}, bf16[32,32,768]{2,1,0:T(8,128)(2,1)S(1)}) custom-call(s32[1]{0:T(128)} %bitcast.half_ref, bf16[128,12288]{1,0:T(8,128)(2,1)S(1)} %copy-done, bf16[32,16,768]{2,1,0:T(8,128)(2,1)S(1)} %collective-permute-done.rows_ref, f32[64,128]{1,0:T(8,128)S(1)} %shard_map.60.own_ref, bf16[64,128]{1,0:T(8,128)(2,1)S(1)} %bitcast.3), custom_call_target="tpu_custom_call" | custom-call | tf_op jit(solution)/shard_map/pallas_call | solution.py:140
  48.0 46.0 %all_to_all.16.got_ref = bf16[32,32,768]{2,1,0:T(8,128)(2,1)S(1)} all-to-all(bf16[32,32,768]{2,1,0:T(8,128)(2,1)S(1)} %get-tuple-element.5), channel_id=1, replica_groups=mesh['node'=32,'y'=4,'pair'=4,'parity'=2] {'y','pair','parity'}, dimensions={0} | all-to-all | bytes 3145728 | tf_op jit(solution)/shard_map/all_to_all | solution.py:146
  94.0 0.3 shard_map.62
  94.3 28.3 %all_to_all.17 = bf16[32,3,256]{2,1,0:T(4,128)(2,1)S(1)} all-to-all(bf16[32,3,256]{2,1,0:T(4,128)(2,1)S(1)} %shard_map.62), channel_id=1, replica_groups=mesh['node'=32,'y'=4,'pair'=4,'parity'=2] {'node'}, dimensions={0} | all-to-all | bytes 98304 | tf_op jit(solution)/shard_map/all_to_all | solution.py:150
  122.6 0.6 convert_reduce_fusion
Async XLA Ops:
  0.6 0.8 copy-start.1
  1.4 0.7 copy-start.3
  34.8 10.9 %collective-permute-start = (bf16[32,16,768]{2,1,0:T(8,128)(2,1)S(1)}, bf16[32,16,768]{2,1,0:T(8,128)(2,1)S(1)}, u32[]{:S(2)}, u32[]{:S(2)}) collective-permute-start(bf16[32,16,768]{2,1,0:T(8,128)(2,1)S(1)} %all_to_all.15.rows_ref), channel_id=1, source_target_pairs={{0,32},{32,0},{64,96},{96,64},{128,160},{160,128},{192,224},{224,1... | collective-permute-start | bytes 2359304 | tf_op jit(solution)/shard_map/ppermute | solution.py:136
  42.7 1.9 %copy-start = (bf16[128,12288]{1,0:T(8,128)(2,1)S(1)}, bf16[128,12288]{1,0:T(8,128)(2,1)}, u32[]{:S(2)}) copy-start(bf16[128,12288]{1,0:T(8,128)(2,1)} %tokens_ref.3) | copy-start | bytes 9437188
  44.6 1.1 copy-start.2

commit v3 on v2

--- a/solution.py
+++ b/solution.py
@@ -82,7 +82,7 @@
     out_ref[...] = before_half(half_ref[0], tokens_ref, rows_ref)
 
 
-def first_kernel(half_ref, tokens_ref, rows_ref, own_ref, cot_ref, act_ref, sent_ref):
+def first_kernel(half_ref, parity_ref, tokens_ref, rows_ref, own_ref, cot_ref, act_ref, sent_ref):
     before = own_ref[...] + before_half(1 - half_ref[0], tokens_ref, rows_ref)
     tanh_inner = jnp.tanh(TANH_SCALE * (before + CUBIC_TERM * before * before * before))
     act_ref[...] = (0.5 * before * (1.0 + tanh_inner)).astype(jnp.bfloat16)
@@ -97,15 +97,19 @@
     slope = jnp.dot(
         jnp.where(pick, 1.0, 0.0).astype(jnp.bfloat16), slope, preferred_element_type=jnp.float32
     ).astype(jnp.bfloat16)
-    nodes = slope.shape[0] // 2
-    per_row = RING_Y * RING_X // 2
-    piece = tokens_ref.shape[1] // per_row
-    for i in range(per_row):
+    slots, nodes, piece = sent_ref.shape[1:]
+    for i in range(slots):
         partial = jnp.dot(slope, tokens_ref[:, i * piece : (i + 1) * piece], preferred_element_type=jnp.float32)
         value = clip_blocks(partial)
         for row_parity in range(2):
-            owner = row_parity * per_row + i
-            sent_ref[owner] = value[row_parity * nodes : (row_parity + 1) * nodes]
+            owner = row_parity * slots + i
+            sent_ref[(owner + parity_ref[0]) % 2, owner // 2] = value[row_parity * nodes : (row_parity + 1) * nodes]
+
+
+def pair_kernel(kept_ref, got_ref, out_ref):
+    for slot in range(out_ref.shape[0]):
+        total = kept_ref[0, slot].astype(jnp.float32) + got_ref[slot].astype(jnp.float32)
+        out_ref[slot] = total.astype(jnp.bfloat16)
 
 
 def group_kernel(got_ref, out_ref):
@@ -123,7 +127,6 @@
     own_rows = weight_q.shape[0]
     hidden = cotangent.shape[1]
     piece = hidden * depth // (node_count * local_count)
-    side = node_count // 2
     half = (lax.axis_index("node") % 2).astype(jnp.int32).reshape(1)
     parity = lax.axis_index("parity").astype(jnp.int32).reshape(1)
     call = functools.partial(pl.pallas_call, compiler_params=PARAMS)
@@ -137,13 +140,22 @@
     before = call(
         own_kernel, out_shape=shape((hidden, batch), jnp.float32), in_specs=[SMEM, VMEM, VMEM], out_specs=VMEM
     )(half, tokens, own)
-    activation, sent = call(
+    activation, parts = call(
         first_kernel,
-        out_shape=(shape((hidden, batch)), shape((local_count, node_count, piece))),
-        in_specs=[SMEM] + [VMEM] * 4,
+        out_shape=(shape((hidden, batch)), shape((2, local_count // 2, node_count, piece))),
+        in_specs=[SMEM] * 2 + [VMEM] * 4,
         out_specs=(VMEM,) * 2,
-    )(half, tokens, other, before, cotangent.T)
-    got = lax.all_to_all(sent, ("y", "pair", "parity"), split_axis=0, concat_axis=0, tiled=True)
+    )(half, parity, tokens, other, before, cotangent.T)
+    partners = [
+        (n * RING_X + x, n * RING_X + (x + (1 if (x + n) % 2 == 0 else -1)) % RING_X)
+        for n in range(node_count)
+        for x in range(RING_X)
+    ]
+    paired = lax.ppermute(parts[1], ("node", "pair", "parity"), partners)
+    sent = call(
+        pair_kernel, out_shape=shape((local_count // 2, node_count, piece)), in_specs=[VMEM] * 2, out_specs=VMEM
+    )(parts, paired)
+    got = lax.all_to_all(sent, ("y", "pair"), split_axis=0, concat_axis=0, tiled=True)
     group = call(
         group_kernel, out_shape=shape((node_count, piece // BLOCK, BLOCK)), in_specs=[VMEM], out_specs=VMEM
     )(got)

time: 124 us -> 122 us (0.984)
  blocking collectives: 107 us -> 90.6 us
  waiting for transfers between devices: 0.01 us -> 11 us
  starting transfers between devices: 7.88 us -> 10.9 us
    all_to_all x1, blocking collectives: 46 us -> 30.8 us  [per_device(): lax.all_to_all(sent, ('y', 'pair'), split_axis=0, concat_axis=0, tiled=True)]
    ppermute x0 -> x1, waiting for transfers between devices: none -> 11 us  [per_device(): paired = lax.ppermute(parts[1], ('node', 'pair', 'parity'), partners)]
    ppermute x0 -> x1, starting transfers between devices: none -> 2.97 us  [per_device(): paired = lax.ppermute(parts[1], ('node', 'pair', 'parity'), partners)]
    pallas_call x1 -> x2, Pallas kernels: 2.31 us -> 2.96 us  [the longest x1 2.78 us: per_device(): call(first_kernel, out_shape=(shape((hidden, batch)), shape((2, local_cou...]
  transfers between devices with their start and end apart: 1 -> 2, of which waited for: 0 -> 1; matrix products, arithmetic and copies ran while one was open for 0% -> 0% of each run, Pallas kernels for 1% -> 1%
where the time goes in v3:
time: 122 us
  blocking collectives  90.6 us (74%)
  waiting for transfers between devices  11 us (9%)
  starting transfers between devices  10.9 us (9%)
  Pallas kernels  4.44 us (4%)
  local copies, waits for them, and re-layouts  3.39 us (3%)
    all_to_all x1, blocking collectives, per_device(): lax.all_to_all(copies, ('y', 'pair', 'parity'), split_axis=0, concat_axis...  32.5 us
    all_to_all x1, blocking collectives, per_device(): lax.all_to_all(sent, ('y', 'pair'), split_axis=0, concat_axis=0, tiled=True)  30.8 us
    all_to_all x1, blocking collectives, per_device(): got = lax.all_to_all(group, 'node', split_axis=0, concat_axis=0, tiled=True)  27.3 us
    ppermute x1, waiting for transfers between devices, per_device(): paired = lax.ppermute(parts[1], ('node', 'pair', 'parity'), partners)  11 us
    ppermute x1, starting transfers between devices, per_device(): other = lax.ppermute(own, 'node', [(n, n ^ 1) for n in range(node_count)])  7.88 us
    unnamed x8, local copies, waits for them, and re-layouts  3.33 us
    ppermute x1, starting transfers between devices, per_device(): paired = lax.ppermute(parts[1], ('node', 'pair', 'parity'), partners)  2.97 us
    pallas_call x1, Pallas kernels, per_device(): call(first_kernel, out_shape=(shape((hidden, batch)), shape((2, local_cou...  2.78 us
  transfers between devices with their start and end apart: 2, of which 1 were waited for; matrix products, arithmetic and copies ran while one was open for 0% of the time, Pallas kernels for 1%

profile of v3, /device:TPU:1, one launch (start us, length us, event | category | flops | bytes accessed | tf_op | source)
XLA Modules:
  0.0 121.6 jit_solution(14986171513082614305)
XLA Ops:
  0.6 0.0 copy-start.1
  0.7 0.8 copy-done.1
  1.4 0.0 copy-start.3
  1.4 0.7 copy-done.3
  2.1 0.2 shard_map.59
  2.3 32.5 %all_to_all.15.rows_ref = bf16[32,16,768]{2,1,0:T(8,128)(2,1)S(1)} all-to-all(bf16[32,16,768]{2,1,0:T(8,128)(2,1)S(1)} %shard_map.59), channel_id=1, replica_groups=mesh['node'=32,'y'=4,'pair'=4,'parity'=2] {'y','pair','parity'}, dimensions={0} | all-to-all | bytes 1572864 | tf_op jit(solution)/shard_map/all_to_all | solution.py:138
  34.8 7.9 %collective-permute-start = (bf16[32,16,768]{2,1,0:T(8,128)(2,1)S(1)}, bf16[32,16,768]{2,1,0:T(8,128)(2,1)S(1)}, u32[]{:S(2)}, u32[]{:S(2)}) collective-permute-start(bf16[32,16,768]{2,1,0:T(8,128)(2,1)S(1)} %all_to_all.15.rows_ref), channel_id=1, source_target_pairs={{0,32},{32,0},{64,96},{96,64},{128,160},{160,128},{192,224},{224,1... | collective-permute-start | bytes 2359304 | tf_op jit(solution)/shard_map/ppermute | solution.py:139
  42.7 0.0 copy-start
  42.7 1.9 %copy-done = bf16[128,12288]{1,0:T(8,128)(2,1)S(1)} copy-done((bf16[128,12288]{1,0:T(8,128)(2,1)S(1)}, bf16[128,12288]{1,0:T(8,128)(2,1)}, u32[]{:S(2)}) %copy-start) | copy-done | bytes 3145752
  44.6 0.0 copy-start.2
  44.6 1.1 shard_map.60.own_ref
  45.7 0.0 collective-permute-done.rows_ref
  45.7 0.0 copy-done.2
  45.7 2.8 %shard_map.61 = (bf16[64,128]{1,0:T(8,128)(2,1)}, bf16[2,16,32,768]{3,2,1,0:T(8,128)(2,1)S(1)}) custom-call(s32[1]{0:T(128)} %bitcast.half_ref, s32[1]{0:T(128)} %bitcast.1.parity_ref, bf16[128,12288]{1,0:T(8,128)(2,1)S(1)} %copy-done, bf16[32,16,768]{2,1,0:T(8,128)(2,1)S(1)} %collective-permute-done.rows_ref, f32[64,128]{1,0:T(8,128)S(1)} %shard_map.60.own_ref, ...), custom_call_target="tpu_custom_call" | custom-call | tf_op jit(solution)/shard_map/pallas_call | solution.py:143
  48.5 0.1 slice_bitcast_fusion
  48.5 3.0 %collective-permute-start.1 = (bf16[16,32,768]{2,1,0:T(8,128)(2,1)S(1)}, bf16[16,32,768]{2,1,0:T(8,128)(2,1)S(1)}, u32[]{:S(2)}, u32[]{:S(2)}) collective-permute-start(bf16[16,32,768]{2,1,0:T(8,128)(2,1)S(1)} %slice_bitcast_fusion), channel_id=1, source_target_pairs={{0,1},{1,0},{2,3},{3,2},{4,5},{5,4},{6,7},{7,6},{32,39},{33,34},{3... | collective-permute-start | bytes 2359304 | tf_op jit(solution)/shard_map/ppermute | solution.py:154
  51.5 11.0 %collective-permute-done.1.got_ref = bf16[16,32,768]{2,1,0:T(8,128)(2,1)S(1)} collective-permute-done((bf16[16,32,768]{2,1,0:T(8,128)(2,1)S(1)}, bf16[16,32,768]{2,1,0:T(8,128)(2,1)S(1)}, u32[]{:S(2)}, u32[]{:S(2)}) %collective-permute-start.1) | collective-permute-done | bytes 786464 | tf_op jit(solution)/shard_map/ppermute | solution.py:154
  62.5 0.2 shard_map.62
  62.6 30.8 %all_to_all.16.got_ref = bf16[16,32,768]{2,1,0:T(8,128)(2,1)S(1)} all-to-all(bf16[16,32,768]{2,1,0:T(8,128)(2,1)S(1)} %shard_map.62), channel_id=1, replica_groups=mesh['node'=32,'y'=4,'pair'=4,'parity'=2] {'y','pair'}, dimensions={0} | all-to-all | bytes 1572864 | tf_op jit(solution)/shard_map/all_to_all | solution.py:158
  93.4 0.2 shard_map.63
  93.6 27.3 %all_to_all.17 = bf16[32,3,256]{2,1,0:T(4,128)(2,1)S(1)} all-to-all(bf16[32,3,256]{2,1,0:T(4,128)(2,1)S(1)} %shard_map.63), channel_id=1, replica_groups=mesh['node'=32,'y'=4,'pair'=4,'parity'=2] {'node'}, dimensions={0} | all-to-all | bytes 98304 | tf_op jit(solution)/shard_map/all_to_all | solution.py:162
  120.9 0.6 convert_reduce_fusion
Async XLA Ops:
  0.6 0.8 copy-start.1
  1.4 0.7 copy-start.3
  34.8 10.9 %collective-permute-start = (bf16[32,16,768]{2,1,0:T(8,128)(2,1)S(1)}, bf16[32,16,768]{2,1,0:T(8,128)(2,1)S(1)}, u32[]{:S(2)}, u32[]{:S(2)}) collective-permute-start(bf16[32,16,768]{2,1,0:T(8,128)(2,1)S(1)} %all_to_all.15.rows_ref), channel_id=1, source_target_pairs={{0,32},{32,0},{64,96},{96,64},{128,160},{160,128},{192,224},{224,1... | collective-permute-start | bytes 2359304 | tf_op jit(solution)/shard_map/ppermute | solution.py:139
  42.7 1.9 %copy-start = (bf16[128,12288]{1,0:T(8,128)(2,1)S(1)}, bf16[128,12288]{1,0:T(8,128)(2,1)}, u32[]{:S(2)}) copy-start(bf16[128,12288]{1,0:T(8,128)(2,1)} %tokens_ref.3) | copy-start | bytes 9437188
  44.6 1.1 copy-start.2
  48.5 13.9 %collective-permute-start.1 = (bf16[16,32,768]{2,1,0:T(8,128)(2,1)S(1)}, bf16[16,32,768]{2,1,0:T(8,128)(2,1)S(1)}, u32[]{:S(2)}, u32[]{:S(2)}) collective-permute-start(bf16[16,32,768]{2,1,0:T(8,128)(2,1)S(1)} %slice_bitcast_fusion), channel_id=1, source_target_pairs={{0,1},{1,0},{2,3},{3,2},{4,5},{5,4},{6,7},{7,6},{32,39},{33,34},{3... | collective-permute-start | bytes 2359304 | tf_op jit(solution)/shard_map/ppermute | solution.py:154

commit v4 on v3

--- a/solution.py
+++ b/solution.py
@@ -17,10 +17,15 @@
 PARAMS = pltpu.CompilerParams(vmem_limit_bytes=24 * 1024 * 1024)
 VMEM = pl.BlockSpec(memory_space=pltpu.VMEM)
 SMEM = pl.BlockSpec(memory_space=pltpu.SMEM)
+HBM = pl.BlockSpec(memory_space=pltpu.HBM)
 
 
 def shape(dims, dtype=jnp.bfloat16):
     return jax.ShapeDtypeStruct(dims, dtype)
+
+
+def in_hbm(value):
+    return pltpu.with_memory_space_constraint(value, pltpu.HBM)
 
 
 def clip_block(block):
@@ -36,7 +41,15 @@
     )
 
 
-def weight_kernel(half_ref, quant_ref, scale_ref, out_ref):
+def weight_kernel(half_ref, quant_hbm, scale_hbm, out_ref, quant_ref, scale_ref, sems):
+    fetches = [
+        pltpu.make_async_copy(quant_hbm, quant_ref, sems.at[0]),
+        pltpu.make_async_copy(scale_hbm, scale_ref, sems.at[1]),
+    ]
+    for fetch in fetches:
+        fetch.start()
+    for fetch in fetches:
+        fetch.wait()
     own_rows, depth = quant_ref.shape
     width = out_ref.shape[2]
     pieces = depth // 2 // width
@@ -82,7 +95,7 @@
     out_ref[...] = before_half(half_ref[0], tokens_ref, rows_ref)
 
 
-def first_kernel(half_ref, parity_ref, tokens_ref, rows_ref, own_ref, cot_ref, act_ref, sent_ref):
+def first_kernel(half_ref, parity_ref, tokens_ref, rows_ref, own_ref, cot_ref, act_ref, slope_ref, sent_ref):
     before = own_ref[...] + before_half(1 - half_ref[0], tokens_ref, rows_ref)
     tanh_inner = jnp.tanh(TANH_SCALE * (before + CUBIC_TERM * before * before * before))
     act_ref[...] = (0.5 * before * (1.0 + tanh_inner)).astype(jnp.bfloat16)
@@ -97,18 +110,27 @@
     slope = jnp.dot(
         jnp.where(pick, 1.0, 0.0).astype(jnp.bfloat16), slope, preferred_element_type=jnp.float32
     ).astype(jnp.bfloat16)
-    slots, nodes, piece = sent_ref.shape[1:]
-    for i in range(slots):
-        partial = jnp.dot(slope, tokens_ref[:, i * piece : (i + 1) * piece], preferred_element_type=jnp.float32)
+    slope_ref[...] = slope
+    partials(slope, tokens_ref, 1 - parity_ref[0], sent_ref)
+
+
+def second_kernel(parity_ref, tokens_ref, slope_ref, kept_ref):
+    partials(slope_ref[...], tokens_ref, parity_ref[0], kept_ref)
+
+
+def partials(slope, tokens_ref, parity, out_ref):
+    slots, nodes, piece = out_ref.shape
+    for i in range(slots // 2):
+        columns = pl.ds(pl.multiple_of((2 * i + parity) * piece, 128), piece)
+        partial = jnp.dot(slope, tokens_ref[:, columns], preferred_element_type=jnp.float32)
         value = clip_blocks(partial)
-        for row_parity in range(2):
-            owner = row_parity * slots + i
-            sent_ref[(owner + parity_ref[0]) % 2, owner // 2] = value[row_parity * nodes : (row_parity + 1) * nodes]
+        out_ref[i] = value[:nodes]
+        out_ref[slots // 2 + i] = value[nodes:]
 
 
 def pair_kernel(kept_ref, got_ref, out_ref):
     for slot in range(out_ref.shape[0]):
-        total = kept_ref[0, slot].astype(jnp.float32) + got_ref[slot].astype(jnp.float32)
+        total = kept_ref[slot].astype(jnp.float32) + got_ref[slot].astype(jnp.float32)
         out_ref[slot] = total.astype(jnp.bfloat16)
 
 
@@ -131,30 +153,41 @@
     parity = lax.axis_index("parity").astype(jnp.int32).reshape(1)
     call = functools.partial(pl.pallas_call, compiler_params=PARAMS)
 
+    tokens = pltpu.with_memory_space_constraint(tokens, pltpu.VMEM)
     share = shape((local_count, ROWS, own_rows * depth // 2 // ROWS))
-    copies = call(weight_kernel, out_shape=share, in_specs=[SMEM, VMEM, VMEM], out_specs=VMEM)(
-        half, weight_q, weight_scale
-    )
+    copies = call(
+        weight_kernel,
+        out_shape=share,
+        in_specs=[SMEM, HBM, HBM],
+        out_specs=VMEM,
+        scratch_shapes=[
+            pltpu.VMEM(weight_q.shape, weight_q.dtype),
+            pltpu.VMEM(weight_scale.shape, weight_scale.dtype),
+            pltpu.SemaphoreType.DMA((2,)),
+        ],
+    )(half, in_hbm(weight_q), in_hbm(weight_scale))
     own = lax.all_to_all(copies, ("y", "pair", "parity"), split_axis=0, concat_axis=0, tiled=True)
     other = lax.ppermute(own, "node", [(n, n ^ 1) for n in range(node_count)])
     before = call(
         own_kernel, out_shape=shape((hidden, batch), jnp.float32), in_specs=[SMEM, VMEM, VMEM], out_specs=VMEM
     )(half, tokens, own)
-    activation, parts = call(
+    parts = shape((local_count // 2, node_count, piece))
+    activation, slope, sent = call(
         first_kernel,
-        out_shape=(shape((hidden, batch)), shape((2, local_count // 2, node_count, piece))),
+        out_shape=(shape((hidden, batch)), shape((hidden, batch)), parts),
         in_specs=[SMEM] * 2 + [VMEM] * 4,
-        out_specs=(VMEM,) * 2,
+        out_specs=(VMEM,) * 3,
     )(half, parity, tokens, other, before, cotangent.T)
+    kept = call(second_kernel, out_shape=parts, in_specs=[SMEM, VMEM, VMEM], out_specs=VMEM)(parity, tokens, slope)
     partners = [
         (n * RING_X + x, n * RING_X + (x + (1 if (x + n) % 2 == 0 else -1)) % RING_X)
         for n in range(node_count)
         for x in range(RING_X)
     ]
-    paired = lax.ppermute(parts[1], ("node", "pair", "parity"), partners)
+    paired = lax.ppermute(sent, ("node", "pair", "parity"), partners)
     sent = call(
-        pair_kernel, out_shape=shape((local_count // 2, node_count, piece)), in_specs=[VMEM] * 2, out_specs=VMEM
-    )(parts, paired)
+        pair_kernel, out_shape=parts, in_specs=[VMEM] * 2, out_specs=VMEM
+    )(kept, paired)
     got = lax.all_to_all(sent, ("y", "pair"), split_axis=0, concat_axis=0, tiled=True)
     group = call(
         group_kernel, out_shape=shape((node_count, piece // BLOCK, BLOCK)), in_specs=[VMEM], out_specs=VMEM

time: 122 us -> 121 us (level)
  local copies, waits for them, and re-layouts: 3.39 us -> 1.89 us
    unnamed x8 -> x6, local copies, waits for them, and re-layouts: 3.33 us -> 1.89 us
    pallas_call x3 -> x4, Pallas kernels: 3.17 us -> 3.87 us  [the longest x1 2.07 us: per_device(): call(first_kernel, out_shape=(shape((hidden, batch)), shape((hidden, batc...]
where the time goes in v4:
time: 121 us; the launch traced here: 120 us
  blocking collectives  90.6 us (75%)
  starting transfers between devices  10.8 us (9%)
  waiting for transfers between devices  10.4 us (9%)
  Pallas kernels  5.14 us (4%)
  local copies, waits for them, and re-layouts  1.89 us (2%)
    all_to_all x1, blocking collectives, per_device(): lax.all_to_all(copies, ('y', 'pair', 'parity'), split_axis=0, concat_axis...  32.5 us
    all_to_all x1, blocking collectives, per_device(): lax.all_to_all(sent, ('y', 'pair'), split_axis=0, concat_axis=0, tiled=True)  30.8 us
    all_to_all x1, blocking collectives, per_device(): got = lax.all_to_all(group, 'node', split_axis=0, concat_axis=0, tiled=True)  27.2 us
    ppermute x1, waiting for transfers between devices, per_device(): paired = lax.ppermute(sent, ('node', 'pair', 'parity'), partners)  10.4 us
    ppermute x1, starting transfers between devices, per_device(): other = lax.ppermute(own, 'node', [(n, n ^ 1) for n in range(node_count)])  7.88 us
    ppermute x1, starting transfers between devices, per_device(): paired = lax.ppermute(sent, ('node', 'pair', 'parity'), partners)  2.96 us
  transfers between devices with their start and end apart: 2, of which 1 were waited for; matrix products, arithmetic and copies ran while one was open for 0% of the time, Pallas kernels for 1%

profile of v4, /device:TPU:1, one launch (start us, length us, event | category | flops | bytes accessed | tf_op | source)
XLA Modules:
  0.0 120.2 jit_solution(9965913781890398067)
XLA Ops:
  0.6 0.0 copy-start.2
  0.7 1.0 shard_map.59
  1.7 32.5 %all_to_all.15.rows_ref = bf16[32,16,768]{2,1,0:T(8,128)(2,1)S(1)} all-to-all(bf16[32,16,768]{2,1,0:T(8,128)(2,1)S(1)} %shard_map.59), channel_id=1, replica_groups=mesh['node'=32,'y'=4,'pair'=4,'parity'=2] {'y','pair','parity'}, dimensions={0} | all-to-all | bytes 1572864 | tf_op jit(solution)/shard_map/all_to_all | solution.py:169
  34.2 7.9 %collective-permute-start = (bf16[32,16,768]{2,1,0:T(8,128)(2,1)S(1)}, bf16[32,16,768]{2,1,0:T(8,128)(2,1)S(1)}, u32[]{:S(2)}, u32[]{:S(2)}) collective-permute-start(bf16[32,16,768]{2,1,0:T(8,128)(2,1)S(1)} %all_to_all.15.rows_ref), channel_id=1, source_target_pairs={{0,32},{32,0},{64,96},{96,64},{128,160},{160,128},{192,224},{224,1... | collective-permute-start | bytes 2359304 | tf_op jit(solution)/shard_map/ppermute | solution.py:170
  42.1 0.0 copy-start
  42.1 1.9 %copy-done = bf16[128,12288]{1,0:T(8,128)(2,1)S(1)} copy-done((bf16[128,12288]{1,0:T(8,128)(2,1)S(1)}, bf16[128,12288]{1,0:T(8,128)(2,1)}, u32[]{:S(2)}) %copy-start) | copy-done | bytes 3145752
  44.0 0.0 copy-start.1
  44.0 1.1 shard_map.60.own_ref
  45.0 0.0 collective-permute-done.rows_ref
  45.0 0.0 copy-done.2
  45.1 2.1 %shard_map.61 = (bf16[64,128]{1,0:T(8,128)(2,1)}, bf16[64,128]{1,0:T(8,128)(2,1)S(1)}, bf16[16,32,768]{2,1,0:T(8,128)(2,1)S(1)}) custom-call(s32[1]{0:T(128)} %bitcast.half_ref, s32[1]{0:T(128)} %bitcast.1.parity_ref, bf16[128,12288]{1,0:T(8,128)(2,1)S(1)} %copy-done, bf16[32,16,768]{2,1,0:T(8,128)(2,1)S(1)} %collective-permute-done.rows_ref, ...), custom_call_target="tpu_custom_call" | custom-call | tf_op jit(solution)/shard_map/pallas_call | solution.py:175
  47.1 3.0 %collective-permute-start.1 = (bf16[16,32,768]{2,1,0:T(8,128)(2,1)S(1)}, bf16[16,32,768]{2,1,0:T(8,128)(2,1)S(1)}, u32[]{:S(2)}, u32[]{:S(2)}) collective-permute-start(bf16[16,32,768]{2,1,0:T(8,128)(2,1)S(1)} %get-tuple-element.7), channel_id=1, source_target_pairs={{0,1},{1,0},{2,3},{3,2},{4,5},{5,4},{6,7},{7,6},{32,39},{33,34},{3... | collective-permute-start | bytes 2359304 | tf_op jit(solution)/shard_map/ppermute | solution.py:187
  50.1 0.0 copy-done.1
  50.1 0.6 shard_map.62.kept_ref
  50.7 10.4 %collective-permute-done.1.got_ref = bf16[16,32,768]{2,1,0:T(8,128)(2,1)S(1)} collective-permute-done((bf16[16,32,768]{2,1,0:T(8,128)(2,1)S(1)}, bf16[16,32,768]{2,1,0:T(8,128)(2,1)S(1)}, u32[]{:S(2)}, u32[]{:S(2)}) %collective-permute-start.1) | collective-permute-done | bytes 786464 | tf_op jit(solution)/shard_map/ppermute | solution.py:187
  61.1 0.2 shard_map.63
  61.2 30.8 %all_to_all.16.got_ref = bf16[16,32,768]{2,1,0:T(8,128)(2,1)S(1)} all-to-all(bf16[16,32,768]{2,1,0:T(8,128)(2,1)S(1)} %shard_map.63), channel_id=1, replica_groups=mesh['node'=32,'y'=4,'pair'=4,'parity'=2] {'y','pair'}, dimensions={0} | all-to-all | bytes 1572864 | tf_op jit(solution)/shard_map/all_to_all | solution.py:191
  92.1 0.2 shard_map.64
  92.3 27.2 %all_to_all.17 = bf16[32,3,256]{2,1,0:T(4,128)(2,1)S(1)} all-to-all(bf16[32,3,256]{2,1,0:T(4,128)(2,1)S(1)} %shard_map.64), channel_id=1, replica_groups=mesh['node'=32,'y'=4,'pair'=4,'parity'=2] {'node'}, dimensions={0} | all-to-all | bytes 98304 | tf_op jit(solution)/shard_map/all_to_all | solution.py:195
  119.5 0.6 convert_reduce_fusion
Async XLA Ops:
  0.6 44.4 %copy-start.2 = (bf16[128,64]{0,1:T(8,128)(2,1)S(1)}, bf16[128,64]{0,1:T(8,128)(2,1)}, u32[]{:S(2)}) copy-start(bf16[128,64]{0,1:T(8,128)(2,1)} %param.7) | copy-start | bytes 49156
  34.2 10.9 %collective-permute-start = (bf16[32,16,768]{2,1,0:T(8,128)(2,1)S(1)}, bf16[32,16,768]{2,1,0:T(8,128)(2,1)S(1)}, u32[]{:S(2)}, u32[]{:S(2)}) collective-permute-start(bf16[32,16,768]{2,1,0:T(8,128)(2,1)S(1)} %all_to_all.15.rows_ref), channel_id=1, source_target_pairs={{0,32},{32,0},{64,96},{96,64},{128,160},{160,128},{192,224},{224,1... | collective-permute-start | bytes 2359304 | tf_op jit(solution)/shard_map/ppermute | solution.py:170
  42.1 1.9 %copy-start = (bf16[128,12288]{1,0:T(8,128)(2,1)S(1)}, bf16[128,12288]{1,0:T(8,128)(2,1)}, u32[]{:S(2)}) copy-start(bf16[128,12288]{1,0:T(8,128)(2,1)} %tokens_ref.5) | copy-start | bytes 9437188
  44.0 6.1 %copy-start.1 = (bf16[128,12288]{1,0:T(8,128)(2,1)S(1)}, bf16[128,12288]{1,0:T(8,128)(2,1)}, u32[]{:S(2)}) copy-start(bf16[128,12288]{1,0:T(8,128)(2,1)} %tokens_ref.5) | copy-start | bytes 9437188
  47.1 13.9 %collective-permute-start.1 = (bf16[16,32,768]{2,1,0:T(8,128)(2,1)S(1)}, bf16[16,32,768]{2,1,0:T(8,128)(2,1)S(1)}, u32[]{:S(2)}, u32[]{:S(2)}) collective-permute-start(bf16[16,32,768]{2,1,0:T(8,128)(2,1)S(1)} %get-tuple-element.7), channel_id=1, source_target_pairs={{0,1},{1,0},{2,3},{3,2},{4,5},{5,4},{6,7},{7,6},{32,39},{33,34},{3... | collective-permute-start | bytes 2359304 | tf_op jit(solution)/shard_map/ppermute | solution.py:187

commit v5 on v4

--- a/solution.py
+++ b/solution.py
@@ -12,7 +12,7 @@
 CLIP_LEVEL = 3.0
 TANH_SCALE = 0.7978845608028654
 CUBIC_TERM = 0.044715
-ROWS = 16
+ROWS = 8
 RING_Y, RING_X = 4, 8
 PARAMS = pltpu.CompilerParams(vmem_limit_bytes=24 * 1024 * 1024)
 VMEM = pl.BlockSpec(memory_space=pltpu.VMEM)

time: 121 us -> 120 us (level)
  no operation moved by 1% of the time
where the time goes in v5:
time: 120 us; the launch traced here: 119 us
  blocking collectives  90.6 us (76%)
  starting transfers between devices  10.8 us (9%)
  waiting for transfers between devices  10.4 us (9%)
  Pallas kernels  4.37 us (4%)
  local copies, waits for them, and re-layouts  1.89 us (2%)
    all_to_all x1, blocking collectives, per_device(): lax.all_to_all(copies, ('y', 'pair', 'parity'), split_axis=0, concat_axis...  32.5 us
    all_to_all x1, blocking collectives, per_device(): lax.all_to_all(sent, ('y', 'pair'), split_axis=0, concat_axis=0, tiled=True)  30.9 us
    all_to_all x1, blocking collectives, per_device(): got = lax.all_to_all(group, 'node', split_axis=0, concat_axis=0, tiled=True)  27.2 us
    ppermute x1, waiting for transfers between devices, per_device(): paired = lax.ppermute(sent, ('node', 'pair', 'parity'), partners)  10.4 us
    ppermute x1, starting transfers between devices, per_device(): other = lax.ppermute(own, 'node', [(n, n ^ 1) for n in range(node_count)])  7.88 us
    ppermute x1, starting transfers between devices, per_device(): paired = lax.ppermute(sent, ('node', 'pair', 'parity'), partners)  2.96 us
  transfers between devices with their start and end apart: 2, of which 1 were waited for; matrix products, arithmetic and copies ran while one was open for 0% of the time, Pallas kernels for 1%

profile of v5, /device:TPU:1, one launch (start us, length us, event | category | flops | bytes accessed | tf_op | source)
XLA Modules:
  0.0 119.4 jit_solution(13298598326509356467)
XLA Ops:
  0.6 0.0 copy-start.2
  0.7 1.0 shard_map.59
  1.7 32.5 %all_to_all.15.rows_ref = bf16[32,8,1536]{2,1,0:T(8,128)(2,1)S(1)} all-to-all(bf16[32,8,1536]{2,1,0:T(8,128)(2,1)S(1)} %shard_map.59), channel_id=1, replica_groups=mesh['node'=32,'y'=4,'pair'=4,'parity'=2] {'y','pair','parity'}, dimensions={0} | all-to-all | bytes 1572864 | tf_op jit(solution)/shard_map/all_to_all | solution.py:169
  34.2 7.9 %collective-permute-start = (bf16[32,8,1536]{2,1,0:T(8,128)(2,1)S(1)}, bf16[32,8,1536]{2,1,0:T(8,128)(2,1)S(1)}, u32[]{:S(2)}, u32[]{:S(2)}) collective-permute-start(bf16[32,8,1536]{2,1,0:T(8,128)(2,1)S(1)} %all_to_all.15.rows_ref), channel_id=1, source_target_pairs={{0,32},{32,0},{64,96},{96,64},{128,160},{160,128},{192,224},{224,1... | collective-permute-start | bytes 2359304 | tf_op jit(solution)/shard_map/ppermute | solution.py:170
  42.1 0.0 copy-start
  42.1 1.9 %copy-done = bf16[128,12288]{1,0:T(8,128)(2,1)S(1)} copy-done((bf16[128,12288]{1,0:T(8,128)(2,1)S(1)}, bf16[128,12288]{1,0:T(8,128)(2,1)}, u32[]{:S(2)}) %copy-start) | copy-done | bytes 3145752
  44.0 0.0 copy-start.1
  44.0 0.7 shard_map.60.own_ref
  44.6 0.0 collective-permute-done.rows_ref
  44.7 0.0 copy-done.2
  44.7 1.7 %shard_map.61 = (bf16[64,128]{1,0:T(8,128)(2,1)}, bf16[64,128]{1,0:T(8,128)(2,1)S(1)}, bf16[16,32,768]{2,1,0:T(8,128)(2,1)S(1)}) custom-call(s32[1]{0:T(128)} %bitcast.half_ref, s32[1]{0:T(128)} %bitcast.1.parity_ref, bf16[128,12288]{1,0:T(8,128)(2,1)S(1)} %copy-done, bf16[32,8,1536]{2,1,0:T(8,128)(2,1)S(1)} %collective-permute-done.rows_ref, ...), custom_call_target="tpu_custom_call" | custom-call | tf_op jit(solution)/shard_map/pallas_call | solution.py:175
  46.4 3.0 %collective-permute-start.1 = (bf16[16,32,768]{2,1,0:T(8,128)(2,1)S(1)}, bf16[16,32,768]{2,1,0:T(8,128)(2,1)S(1)}, u32[]{:S(2)}, u32[]{:S(2)}) collective-permute-start(bf16[16,32,768]{2,1,0:T(8,128)(2,1)S(1)} %get-tuple-element.7), channel_id=1, source_target_pairs={{0,1},{1,0},{2,3},{3,2},{4,5},{5,4},{6,7},{7,6},{32,39},{33,34},{3... | collective-permute-start | bytes 2359304 | tf_op jit(solution)/shard_map/ppermute | solution.py:187
  49.3 0.0 copy-done.1
  49.3 0.6 shard_map.62.kept_ref
  49.9 10.4 %collective-permute-done.1.got_ref = bf16[16,32,768]{2,1,0:T(8,128)(2,1)S(1)} collective-permute-done((bf16[16,32,768]{2,1,0:T(8,128)(2,1)S(1)}, bf16[16,32,768]{2,1,0:T(8,128)(2,1)S(1)}, u32[]{:S(2)}, u32[]{:S(2)}) %collective-permute-start.1) | collective-permute-done | bytes 786464 | tf_op jit(solution)/shard_map/ppermute | solution.py:187
  60.3 0.2 shard_map.63
  60.5 30.9 %all_to_all.16.got_ref = bf16[16,32,768]{2,1,0:T(8,128)(2,1)S(1)} all-to-all(bf16[16,32,768]{2,1,0:T(8,128)(2,1)S(1)} %shard_map.63), channel_id=1, replica_groups=mesh['node'=32,'y'=4,'pair'=4,'parity'=2] {'y','pair'}, dimensions={0} | all-to-all | bytes 1572864 | tf_op jit(solution)/shard_map/all_to_all | solution.py:191
  91.3 0.2 shard_map.64
  91.5 27.2 %all_to_all.17 = bf16[32,3,256]{2,1,0:T(4,128)(2,1)S(1)} all-to-all(bf16[32,3,256]{2,1,0:T(4,128)(2,1)S(1)} %shard_map.64), channel_id=1, replica_groups=mesh['node'=32,'y'=4,'pair'=4,'parity'=2] {'node'}, dimensions={0} | all-to-all | bytes 98304 | tf_op jit(solution)/shard_map/all_to_all | solution.py:195
  118.8 0.6 convert_reduce_fusion
Async XLA Ops:
  0.6 44.0 %copy-start.2 = (bf16[128,64]{0,1:T(8,128)(2,1)S(1)}, bf16[128,64]{0,1:T(8,128)(2,1)}, u32[]{:S(2)}) copy-start(bf16[128,64]{0,1:T(8,128)(2,1)} %param.7) | copy-start | bytes 49156
  34.2 10.5 %collective-permute-start = (bf16[32,8,1536]{2,1,0:T(8,128)(2,1)S(1)}, bf16[32,8,1536]{2,1,0:T(8,128)(2,1)S(1)}, u32[]{:S(2)}, u32[]{:S(2)}) collective-permute-start(bf16[32,8,1536]{2,1,0:T(8,128)(2,1)S(1)} %all_to_all.15.rows_ref), channel_id=1, source_target_pairs={{0,32},{32,0},{64,96},{96,64},{128,160},{160,128},{192,224},{224,1... | collective-permute-start | bytes 2359304 | tf_op jit(solution)/shard_map/ppermute | solution.py:170
  42.1 1.9 %copy-start = (bf16[128,12288]{1,0:T(8,128)(2,1)S(1)}, bf16[128,12288]{1,0:T(8,128)(2,1)}, u32[]{:S(2)}) copy-start(bf16[128,12288]{1,0:T(8,128)(2,1)} %tokens_ref.5) | copy-start | bytes 9437188
  44.0 5.4 %copy-start.1 = (bf16[128,12288]{1,0:T(8,128)(2,1)S(1)}, bf16[128,12288]{1,0:T(8,128)(2,1)}, u32[]{:S(2)}) copy-start(bf16[128,12288]{1,0:T(8,128)(2,1)} %tokens_ref.5) | copy-start | bytes 9437188
  46.4 13.9 %collective-permute-start.1 = (bf16[16,32,768]{2,1,0:T(8,128)(2,1)S(1)}, bf16[16,32,768]{2,1,0:T(8,128)(2,1)S(1)}, u32[]{:S(2)}, u32[]{:S(2)}) collective-permute-start(bf16[16,32,768]{2,1,0:T(8,128)(2,1)S(1)} %get-tuple-element.7), channel_id=1, source_target_pairs={{0,1},{1,0},{2,3},{3,2},{4,5},{5,4},{6,7},{7,6},{32,39},{33,34},{3... | collective-permute-start | bytes 2359304 | tf_op jit(solution)/shard_map/ppermute | solution.py:187

commit v6 on v5

--- a/solution.py
+++ b/solution.py
@@ -95,10 +95,10 @@
     out_ref[...] = before_half(half_ref[0], tokens_ref, rows_ref)
 
 
-def first_kernel(half_ref, parity_ref, tokens_ref, rows_ref, own_ref, cot_ref, act_ref, slope_ref, sent_ref):
+def first_kernel(half_ref, parity_ref, tokens_ref, rows_ref, own_ref, cot_ref, before_ref, slope_ref, sent_ref):
     before = own_ref[...] + before_half(1 - half_ref[0], tokens_ref, rows_ref)
+    before_ref[...] = before
     tanh_inner = jnp.tanh(TANH_SCALE * (before + CUBIC_TERM * before * before * before))
-    act_ref[...] = (0.5 * before * (1.0 + tanh_inner)).astype(jnp.bfloat16)
     slope = 0.5 * (1.0 + tanh_inner) + 0.5 * before * (1.0 - tanh_inner * tanh_inner) * TANH_SCALE * (
         1.0 + 3.0 * CUBIC_TERM * before * before
     )
@@ -114,7 +114,10 @@
     partials(slope, tokens_ref, 1 - parity_ref[0], sent_ref)
 
 
-def second_kernel(parity_ref, tokens_ref, slope_ref, kept_ref):
+def second_kernel(parity_ref, tokens_ref, before_ref, slope_ref, act_ref, kept_ref):
+    before = before_ref[...]
+    tanh_inner = jnp.tanh(TANH_SCALE * (before + CUBIC_TERM * before * before * before))
+    act_ref[...] = (0.5 * before * (1.0 + tanh_inner)).astype(jnp.bfloat16)
     partials(slope_ref[...], tokens_ref, parity_ref[0], kept_ref)
 
 
@@ -172,13 +175,18 @@
         own_kernel, out_shape=shape((hidden, batch), jnp.float32), in_specs=[SMEM, VMEM, VMEM], out_specs=VMEM
     )(half, tokens, own)
     parts = shape((local_count // 2, node_count, piece))
-    activation, slope, sent = call(
+    before, slope, sent = call(
         first_kernel,
-        out_shape=(shape((hidden, batch)), shape((hidden, batch)), parts),
+        out_shape=(shape((hidden, batch), jnp.float32), shape((hidden, batch)), parts),
         in_specs=[SMEM] * 2 + [VMEM] * 4,
         out_specs=(VMEM,) * 3,
     )(half, parity, tokens, other, before, cotangent.T)
-    kept = call(second_kernel, out_shape=parts, in_specs=[SMEM, VMEM, VMEM], out_specs=VMEM)(parity, tokens, slope)
+    activation, kept = call(
+        second_kernel,
+        out_shape=(shape((hidden, batch)), parts),
+        in_specs=[SMEM] + [VMEM] * 3,
+        out_specs=(VMEM,) * 2,
+    )(parity, tokens, before, slope)
     partners = [
         (n * RING_X + x, n * RING_X + (x + (1 if (x + n) % 2 == 0 else -1)) % RING_X)
         for n in range(node_count)

time: 120 us -> 119 us (level)
  transfers between devices with their start and end apart: 2 -> 2, of which waited for: 1 -> 1; matrix products, arithmetic and copies ran while one was open for 0% -> 0% of each run, Pallas kernels for 1% -> 2%
where the time goes in v6:
time: 119 us
  blocking collectives  90.6 us (76%)
  starting transfers between devices  10.9 us (9%)
  waiting for transfers between devices  9.74 us (8%)
  Pallas kernels  4.69 us (4%)
  local copies, waits for them, and re-layouts  1.89 us (2%)
    all_to_all x1, blocking collectives, per_device(): lax.all_to_all(copies, ('y', 'pair', 'parity'), split_axis=0, concat_axis...  32.5 us
    all_to_all x1, blocking collectives, per_device(): lax.all_to_all(sent, ('y', 'pair'), split_axis=0, concat_axis=0, tiled=True)  30.8 us
    all_to_all x1, blocking collectives, per_device(): got = lax.all_to_all(group, 'node', split_axis=0, concat_axis=0, tiled=True)  27.3 us
    ppermute x1, waiting for transfers between devices, per_device(): paired = lax.ppermute(sent, ('node', 'pair', 'parity'), partners)  9.74 us
    ppermute x1, starting transfers between devices, per_device(): other = lax.ppermute(own, 'node', [(n, n ^ 1) for n in range(node_count)])  7.88 us
    ppermute x1, starting transfers between devices, per_device(): paired = lax.ppermute(sent, ('node', 'pair', 'parity'), partners)  2.98 us
  transfers between devices with their start and end apart: 2, of which 1 were waited for; matrix products, arithmetic and copies ran while one was open for 0% of the time, Pallas kernels for 2%

profile of v6, /device:TPU:1, one launch (start us, length us, event | category | flops | bytes accessed | tf_op | source)
XLA Modules:
  0.0 119.1 jit_solution(17036076664914181192)
XLA Ops:
  0.6 0.0 copy-start.2
  0.7 1.0 shard_map.59
  1.7 32.5 %all_to_all.15.rows_ref = bf16[32,8,1536]{2,1,0:T(8,128)(2,1)S(1)} all-to-all(bf16[32,8,1536]{2,1,0:T(8,128)(2,1)S(1)} %shard_map.59), channel_id=1, replica_groups=mesh['node'=32,'y'=4,'pair'=4,'parity'=2] {'y','pair','parity'}, dimensions={0} | all-to-all | bytes 1572864 | tf_op jit(solution)/shard_map/all_to_all | solution.py:172
  34.2 7.9 %collective-permute-start = (bf16[32,8,1536]{2,1,0:T(8,128)(2,1)S(1)}, bf16[32,8,1536]{2,1,0:T(8,128)(2,1)S(1)}, u32[]{:S(2)}, u32[]{:S(2)}) collective-permute-start(bf16[32,8,1536]{2,1,0:T(8,128)(2,1)S(1)} %all_to_all.15.rows_ref), channel_id=1, source_target_pairs={{0,32},{32,0},{64,96},{96,64},{128,160},{160,128},{192,224},{224,1... | collective-permute-start | bytes 2359304 | tf_op jit(solution)/shard_map/ppermute | solution.py:173
  42.1 0.0 copy-start
  42.1 1.9 %copy-done = bf16[128,12288]{1,0:T(8,128)(2,1)S(1)} copy-done((bf16[128,12288]{1,0:T(8,128)(2,1)S(1)}, bf16[128,12288]{1,0:T(8,128)(2,1)}, u32[]{:S(2)}) %copy-start) | copy-done | bytes 3145752
  44.0 0.0 copy-start.1
  44.0 0.7 shard_map.60.own_ref
  44.6 0.0 collective-permute-done.rows_ref
  44.7 0.0 copy-done.2
  44.7 1.4 %shard_map.61 = (f32[64,128]{1,0:T(8,128)S(1)}, bf16[64,128]{1,0:T(8,128)(2,1)S(1)}, bf16[16,32,768]{2,1,0:T(8,128)(2,1)S(1)}) custom-call(s32[1]{0:T(128)} %bitcast.1.half_ref, s32[1]{0:T(128)} %bitcast.parity_ref, bf16[128,12288]{1,0:T(8,128)(2,1)S(1)} %copy-done, bf16[32,8,1536]{2,1,0:T(8,128)(2,1)S(1)} %collective-permute-done.rows_ref, ...), custom_call_target="tpu_custom_call" | custom-call | tf_op jit(solution)/shard_map/pallas_call | solution.py:178
  46.1 3.0 %collective-permute-start.1 = (bf16[16,32,768]{2,1,0:T(8,128)(2,1)S(1)}, bf16[16,32,768]{2,1,0:T(8,128)(2,1)S(1)}, u32[]{:S(2)}, u32[]{:S(2)}) collective-permute-start(bf16[16,32,768]{2,1,0:T(8,128)(2,1)S(1)} %get-tuple-element.11), channel_id=1, source_target_pairs={{0,1},{1,0},{2,3},{3,2},{4,5},{5,4},{6,7},{7,6},{32,39},{33,34},{3... | collective-permute-start | bytes 2359304 | tf_op jit(solution)/shard_map/ppermute | solution.py:195
  49.0 0.0 copy-done.1
  49.1 1.2 %shard_map.62 = (bf16[64,128]{1,0:T(8,128)(2,1)}, bf16[16,32,768]{2,1,0:T(8,128)(2,1)S(1)}) custom-call(s32[1]{0:T(128)} %bitcast.parity_ref, bf16[128,12288]{1,0:T(8,128)(2,1)S(1)} %copy-done.1, f32[64,128]{1,0:T(8,128)S(1)} %get-tuple-element.7.before_ref, bf16[64,128]{1,0:T(8,128)(2,1)S(1)} %get-tuple-element.8.slope_ref), custom_call_target="tpu_custom_call" | custom-call | tf_op jit(solution)/shard_map/pallas_call | solution.py:184
  50.3 9.7 %collective-permute-done.1.got_ref = bf16[16,32,768]{2,1,0:T(8,128)(2,1)S(1)} collective-permute-done((bf16[16,32,768]{2,1,0:T(8,128)(2,1)S(1)}, bf16[16,32,768]{2,1,0:T(8,128)(2,1)S(1)}, u32[]{:S(2)}, u32[]{:S(2)}) %collective-permute-start.1) | collective-permute-done | bytes 786464 | tf_op jit(solution)/shard_map/ppermute | solution.py:195
  60.0 0.2 shard_map.63
  60.2 30.8 %all_to_all.16.got_ref = bf16[16,32,768]{2,1,0:T(8,128)(2,1)S(1)} all-to-all(bf16[16,32,768]{2,1,0:T(8,128)(2,1)S(1)} %shard_map.63), channel_id=1, replica_groups=mesh['node'=32,'y'=4,'pair'=4,'parity'=2] {'y','pair'}, dimensions={0} | all-to-all | bytes 1572864 | tf_op jit(solution)/shard_map/all_to_all | solution.py:199
  91.0 0.2 shard_map.64
  91.2 27.3 %all_to_all.17 = bf16[32,3,256]{2,1,0:T(4,128)(2,1)S(1)} all-to-all(bf16[32,3,256]{2,1,0:T(4,128)(2,1)S(1)} %shard_map.64), channel_id=1, replica_groups=mesh['node'=32,'y'=4,'pair'=4,'parity'=2] {'node'}, dimensions={0} | all-to-all | bytes 98304 | tf_op jit(solution)/shard_map/all_to_all | solution.py:203
  118.5 0.6 convert_reduce_fusion
Async XLA Ops:
  0.6 44.0 %copy-start.2 = (bf16[128,64]{0,1:T(8,128)(2,1)S(1)}, bf16[128,64]{0,1:T(8,128)(2,1)}, u32[]{:S(2)}) copy-start(bf16[128,64]{0,1:T(8,128)(2,1)} %param.7) | copy-start | bytes 49156
  34.2 10.5 %collective-permute-start = (bf16[32,8,1536]{2,1,0:T(8,128)(2,1)S(1)}, bf16[32,8,1536]{2,1,0:T(8,128)(2,1)S(1)}, u32[]{:S(2)}, u32[]{:S(2)}) collective-permute-start(bf16[32,8,1536]{2,1,0:T(8,128)(2,1)S(1)} %all_to_all.15.rows_ref), channel_id=1, source_target_pairs={{0,32},{32,0},{64,96},{96,64},{128,160},{160,128},{192,224},{224,1... | collective-permute-start | bytes 2359304 | tf_op jit(solution)/shard_map/ppermute | solution.py:173
  42.1 1.9 %copy-start = (bf16[128,12288]{1,0:T(8,128)(2,1)S(1)}, bf16[128,12288]{1,0:T(8,128)(2,1)}, u32[]{:S(2)}) copy-start(bf16[128,12288]{1,0:T(8,128)(2,1)} %tokens_ref.5) | copy-start | bytes 9437188
  44.0 5.1 %copy-start.1 = (bf16[128,12288]{1,0:T(8,128)(2,1)S(1)}, bf16[128,12288]{1,0:T(8,128)(2,1)}, u32[]{:S(2)}) copy-start(bf16[128,12288]{1,0:T(8,128)(2,1)} %tokens_ref.5) | copy-start | bytes 9437188
  46.1 13.9 %collective-permute-start.1 = (bf16[16,32,768]{2,1,0:T(8,128)(2,1)S(1)}, bf16[16,32,768]{2,1,0:T(8,128)(2,1)S(1)}, u32[]{:S(2)}, u32[]{:S(2)}) collective-permute-start(bf16[16,32,768]{2,1,0:T(8,128)(2,1)S(1)} %get-tuple-element.11), channel_id=1, source_target_pairs={{0,1},{1,0},{2,3},{3,2},{4,5},{5,4},{6,7},{7,6},{32,39},{33,34},{3... | collective-permute-start | bytes 2359304 | tf_op jit(solution)/shard_map/ppermute | solution.py:195

commit v7 on v6

--- a/solution.py
+++ b/solution.py
@@ -88,10 +88,20 @@
         )
         total = total + jnp.where(which == c, product[:, :batch], 0.0)
         total = total + jnp.where(which == c + 1, product[:, batch:], 0.0)
-    return jnp.sum(total.reshape(count // pieces, pieces, batch), axis=1)
-
-
-def own_kernel(half_ref, tokens_ref, rows_ref, out_ref):
+    total = total.reshape(count // ROWS, ROWS, batch)
+    return jnp.concatenate([jnp.sum(total[:, :pieces], axis=1), jnp.sum(total[:, pieces:], axis=1)], axis=0)
+
+
+def reorder(rows, back):
+    count = rows.shape[0]
+    number = lax.broadcasted_iota(jnp.int32, (count, count), 0 if back else 1)
+    place = lax.broadcasted_iota(jnp.int32, (count, count), 1 if back else 0)
+    pick = jnp.where(number == place % (count // 2) * 2 + place // (count // 2), 1.0, 0.0).astype(jnp.bfloat16)
+    return jnp.dot(pick, rows, preferred_element_type=jnp.float32).astype(jnp.bfloat16)
+
+
+def own_kernel(half_ref, tokens_ref, rows_ref, cot_ref, out_ref, sorted_ref):
+    sorted_ref[...] = reorder(cot_ref[...], False)
     out_ref[...] = before_half(half_ref[0], tokens_ref, rows_ref)
 
 
@@ -103,13 +113,6 @@
         1.0 + 3.0 * CUBIC_TERM * before * before
     )
     slope = (cot_ref[...].astype(jnp.float32) * slope).astype(jnp.bfloat16)
-    hidden = slope.shape[0]
-    to = lax.broadcasted_iota(jnp.int32, (hidden, hidden), 0)
-    source = lax.broadcasted_iota(jnp.int32, (hidden, hidden), 1)
-    pick = source == to % (hidden // 2) * 2 + to // (hidden // 2)
-    slope = jnp.dot(
-        jnp.where(pick, 1.0, 0.0).astype(jnp.bfloat16), slope, preferred_element_type=jnp.float32
-    ).astype(jnp.bfloat16)
     slope_ref[...] = slope
     partials(slope, tokens_ref, 1 - parity_ref[0], sent_ref)
 
@@ -117,7 +120,7 @@
 def second_kernel(parity_ref, tokens_ref, before_ref, slope_ref, act_ref, kept_ref):
     before = before_ref[...]
     tanh_inner = jnp.tanh(TANH_SCALE * (before + CUBIC_TERM * before * before * before))
-    act_ref[...] = (0.5 * before * (1.0 + tanh_inner)).astype(jnp.bfloat16)
+    act_ref[...] = reorder((0.5 * before * (1.0 + tanh_inner)).astype(jnp.bfloat16), True)
     partials(slope_ref[...], tokens_ref, parity_ref[0], kept_ref)
 
 
@@ -171,16 +174,19 @@
     )(half, in_hbm(weight_q), in_hbm(weight_scale))
     own = lax.all_to_all(copies, ("y", "pair", "parity"), split_axis=0, concat_axis=0, tiled=True)
     other = lax.ppermute(own, "node", [(n, n ^ 1) for n in range(node_count)])
-    before = call(
-        own_kernel, out_shape=shape((hidden, batch), jnp.float32), in_specs=[SMEM, VMEM, VMEM], out_specs=VMEM
-    )(half, tokens, own)
+    before, sorted_cot = call(
+        own_kernel,
+        out_shape=(shape((hidden, batch), jnp.float32), shape((hidden, batch))),
+        in_specs=[SMEM] + [VMEM] * 3,
+        out_specs=(VMEM, VMEM),
+    )(half, tokens, own, cotangent.T)
     parts = shape((local_count // 2, node_count, piece))
     before, slope, sent = call(
         first_kernel,
         out_shape=(shape((hidden, batch), jnp.float32), shape((hidden, batch)), parts),
         in_specs=[SMEM] * 2 + [VMEM] * 4,
         out_specs=(VMEM,) * 3,
-    )(half, parity, tokens, other, before, cotangent.T)
+    )(half, parity, tokens, other, before, sorted_cot)
     activation, kept = call(
         second_kernel,
         out_shape=(shape((hidden, batch)), parts),

time: 119 us -> 120 us (level)
  transfers between devices with their start and end apart: 2 -> 2, of which waited for: 1 -> 1; matrix products, arithmetic and copies ran while one was open for 0% -> 0% of each run, Pallas kernels for 2% -> 1%
where the time goes in v7:
time: 120 us
  blocking collectives  90.6 us (76%)
  starting transfers between devices  10.9 us (9%)
  waiting for transfers between devices  10.2 us (8%)
  Pallas kernels  4.14 us (3%)
  local copies, waits for them, and re-layouts  2.61 us (2%)
    all_to_all x1, blocking collectives, per_device(): lax.all_to_all(copies, ('y', 'pair', 'parity'), split_axis=0, concat_axis...  32.5 us
    all_to_all x1, blocking collectives, per_device(): lax.all_to_all(sent, ('y', 'pair'), split_axis=0, concat_axis=0, tiled=True)  30.9 us
    all_to_all x1, blocking collectives, per_device(): got = lax.all_to_all(group, 'node', split_axis=0, concat_axis=0, tiled=True)  27.2 us
    ppermute x1, waiting for transfers between devices, per_device(): paired = lax.ppermute(sent, ('node', 'pair', 'parity'), partners)  10.2 us
    ppermute x1, starting transfers between devices, per_device(): other = lax.ppermute(own, 'node', [(n, n ^ 1) for n in range(node_count)])  7.88 us
    ppermute x1, starting transfers between devices, per_device(): paired = lax.ppermute(sent, ('node', 'pair', 'parity'), partners)  2.97 us
    unnamed x6, local copies, waits for them, and re-layouts  2.61 us
  transfers between devices with their start and end apart: 2, of which 1 were waited for; matrix products, arithmetic and copies ran while one was open for 0% of the time, Pallas kernels for 1%

profile of v7, /device:TPU:1, one launch (start us, length us, event | category | flops | bytes accessed | tf_op | source)
XLA Modules:
  0.0 119.7 jit_solution(11374107724681264867)
XLA Ops:
  0.6 1.0 shard_map.59
  1.7 32.5 %all_to_all.15.rows_ref = bf16[32,8,1536]{2,1,0:T(8,128)(2,1)S(1)} all-to-all(bf16[32,8,1536]{2,1,0:T(8,128)(2,1)S(1)} %shard_map.59), channel_id=1, replica_groups=mesh['node'=32,'y'=4,'pair'=4,'parity'=2] {'y','pair','parity'}, dimensions={0} | all-to-all | bytes 1572864 | tf_op jit(solution)/shard_map/all_to_all | solution.py:175
  34.2 7.9 %collective-permute-start = (bf16[32,8,1536]{2,1,0:T(8,128)(2,1)S(1)}, bf16[32,8,1536]{2,1,0:T(8,128)(2,1)S(1)}, u32[]{:S(2)}, u32[]{:S(2)}) collective-permute-start(bf16[32,8,1536]{2,1,0:T(8,128)(2,1)S(1)} %all_to_all.15.rows_ref), channel_id=1, source_target_pairs={{0,32},{32,0},{64,96},{96,64},{128,160},{160,128},{192,224},{224,1... | collective-permute-start | bytes 2359304 | tf_op jit(solution)/shard_map/ppermute | solution.py:176
  42.1 0.0 copy-start
  42.1 1.9 %copy-done = bf16[128,12288]{1,0:T(8,128)(2,1)S(1)} copy-done((bf16[128,12288]{1,0:T(8,128)(2,1)S(1)}, bf16[128,12288]{1,0:T(8,128)(2,1)}, u32[]{:S(2)}) %copy-start) | copy-done | bytes 3145752
  43.9 0.0 copy-start.2
  44.0 0.7 copy-done.2
  44.7 0.0 copy-start.1
  44.7 0.7 shard_map.60
  45.3 0.0 collective-permute-done.rows_ref
  45.4 1.3 %shard_map.61 = (f32[64,128]{1,0:T(8,128)S(1)}, bf16[64,128]{1,0:T(8,128)(2,1)S(1)}, bf16[16,32,768]{2,1,0:T(8,128)(2,1)S(1)}) custom-call(s32[1]{0:T(128)} %bitcast.1.half_ref, s32[1]{0:T(128)} %bitcast.parity_ref, bf16[128,12288]{1,0:T(8,128)(2,1)S(1)} %copy-done, bf16[32,8,1536]{2,1,0:T(8,128)(2,1)S(1)} %collective-permute-done.rows_ref, ...), custom_call_target="tpu_custom_call" | custom-call | tf_op jit(solution)/shard_map/pallas_call | solution.py:184
  46.6 3.0 %collective-permute-start.1 = (bf16[16,32,768]{2,1,0:T(8,128)(2,1)S(1)}, bf16[16,32,768]{2,1,0:T(8,128)(2,1)S(1)}, u32[]{:S(2)}, u32[]{:S(2)}) collective-permute-start(bf16[16,32,768]{2,1,0:T(8,128)(2,1)S(1)} %get-tuple-element.15), channel_id=1, source_target_pairs={{0,1},{1,0},{2,3},{3,2},{4,5},{5,4},{6,7},{7,6},{32,39},{33,34},{3... | collective-permute-start | bytes 2359304 | tf_op jit(solution)/shard_map/ppermute | solution.py:201
  49.6 0.0 copy-done.1
  49.6 0.8 shard_map.62
  50.4 10.2 %collective-permute-done.1.got_ref = bf16[16,32,768]{2,1,0:T(8,128)(2,1)S(1)} collective-permute-done((bf16[16,32,768]{2,1,0:T(8,128)(2,1)S(1)}, bf16[16,32,768]{2,1,0:T(8,128)(2,1)S(1)}, u32[]{:S(2)}, u32[]{:S(2)}) %collective-permute-start.1) | collective-permute-done | bytes 786464 | tf_op jit(solution)/shard_map/ppermute | solution.py:201
  60.6 0.2 shard_map.63
  60.8 30.9 %all_to_all.16.got_ref = bf16[16,32,768]{2,1,0:T(8,128)(2,1)S(1)} all-to-all(bf16[16,32,768]{2,1,0:T(8,128)(2,1)S(1)} %shard_map.63), channel_id=1, replica_groups=mesh['node'=32,'y'=4,'pair'=4,'parity'=2] {'y','pair'}, dimensions={0} | all-to-all | bytes 1572864 | tf_op jit(solution)/shard_map/all_to_all | solution.py:205
  91.7 0.2 shard_map.64
  91.9 27.2 %all_to_all.17 = bf16[32,3,256]{2,1,0:T(4,128)(2,1)S(1)} all-to-all(bf16[32,3,256]{2,1,0:T(4,128)(2,1)S(1)} %shard_map.64), channel_id=1, replica_groups=mesh['node'=32,'y'=4,'pair'=4,'parity'=2] {'node'}, dimensions={0} | all-to-all | bytes 98304 | tf_op jit(solution)/shard_map/all_to_all | solution.py:209
  119.1 0.6 convert_reduce_fusion
Async XLA Ops:
  34.2 11.2 %collective-permute-start = (bf16[32,8,1536]{2,1,0:T(8,128)(2,1)S(1)}, bf16[32,8,1536]{2,1,0:T(8,128)(2,1)S(1)}, u32[]{:S(2)}, u32[]{:S(2)}) collective-permute-start(bf16[32,8,1536]{2,1,0:T(8,128)(2,1)S(1)} %all_to_all.15.rows_ref), channel_id=1, source_target_pairs={{0,32},{32,0},{64,96},{96,64},{128,160},{160,128},{192,224},{224,1... | collective-permute-start | bytes 2359304 | tf_op jit(solution)/shard_map/ppermute | solution.py:176
  42.1 1.9 %copy-start = (bf16[128,12288]{1,0:T(8,128)(2,1)S(1)}, bf16[128,12288]{1,0:T(8,128)(2,1)}, u32[]{:S(2)}) copy-start(bf16[128,12288]{1,0:T(8,128)(2,1)} %tokens_ref.5) | copy-start | bytes 9437188
  43.9 0.7 copy-start.2
  44.7 5.0 %copy-start.1 = (bf16[128,12288]{1,0:T(8,128)(2,1)S(1)}, bf16[128,12288]{1,0:T(8,128)(2,1)}, u32[]{:S(2)}) copy-start(bf16[128,12288]{1,0:T(8,128)(2,1)} %tokens_ref.5) | copy-start | bytes 9437188
  46.6 13.9 %collective-permute-start.1 = (bf16[16,32,768]{2,1,0:T(8,128)(2,1)S(1)}, bf16[16,32,768]{2,1,0:T(8,128)(2,1)S(1)}, u32[]{:S(2)}, u32[]{:S(2)}) collective-permute-start(bf16[16,32,768]{2,1,0:T(8,128)(2,1)S(1)} %get-tuple-element.15), channel_id=1, source_target_pairs={{0,1},{1,0},{2,3},{3,2},{4,5},{5,4},{6,7},{7,6},{32,39},{33,34},{3... | collective-permute-start | bytes 2359304 | tf_op jit(solution)/shard_map/ppermute | solution.py:201
